TPU v7x, 32 devices: a whole 2x2x4 slice. The times are simulated.
32 devices in a mesh: span: 16 (over z, y, core), head: 2 (over x).
Axes of the slice: x: 2, y: 2, z: 4, core: 2. Of those that a mesh axis runs over, the one named last changes fastest.
Arguments:
- queries: bfloat16 [8192, 6144], P('span', 'head'), may hold values from -16 to 16
- stacked_key_vectors: bfloat16 [8192, 1024], P('span', 'head'), may hold values from -16 to 16
- stacked_value_vectors: bfloat16 [8192, 1024], P('span', 'head'), may hold values from -6 to 6
- out_weight: bfloat16 [6144, 6144], P('head'), may hold values from -0.625 to 0.625
- residual: bfloat16 [8192, 6144], P(('span', 'head')), may hold values from -6 to 6
- gate_table: float32 [32, 6144], replicated, may hold values from 0.25 to 1.75
- noise_step: int32 [16], replicated, may hold values from 0 to 31
- older_count: int32 [16], replicated, may hold values from 0 to 7, as said below
Outputs:
- output: bfloat16 [8192, 6144], P(('span', 'head'))
Inputs may be any that keep to these rules, and one draw needn't show every extreme that they name: older_count[c] is at most c; some span has exactly 7.
All inputs are finite; a program needn't handle non-finite values.
Results may differ from a plain program's by a relative error of at most 0.014.
Values may be sent and summed in bfloat16 or wider, within the bound.
No kernel may reach another device: no remote copies, remote signals or barrier semaphores. Data moves between devices by JAX's collectives and lax.ppermute only.
A program may use at most 192 MiB of HBM per device.

v0:
```python
import math

import jax
import jax.numpy as jnp
from jax import lax
from jax.sharding import PartitionSpec as P

HEAD_SIZE = 128
OLDER_SPAN_LIMIT = 7


def shifted(block, axis, distance):
    devices = range(lax.axis_size(axis))
    route = [(i - distance, i) for i in devices if i - distance in devices]
    return lax.ppermute(block, axis, route)


def on_device(
    queries,
    stacked_key_vectors,
    stacked_value_vectors,
    out_weight,
    residual,
    gate_table,
    noise_step,
    older_count,
):
    span_len = queries.shape[0]
    kv_heads = stacked_key_vectors.shape[1] // HEAD_SIZE
    q_heads = queries.shape[1] // HEAD_SIZE
    query_group_size = q_heads // kv_heads
    my_span = lax.axis_index("span")
    older_mine = older_count[my_span]
    grouped = queries.reshape(span_len, kv_heads, query_group_size, HEAD_SIZE)
    kv_pair = jnp.stack([stacked_key_vectors, stacked_value_vectors])
    score_scale = 1.0 / math.sqrt(HEAD_SIZE)

    def update(carry_state, kv_block):
        running_max, row_total, weighted = carry_state
        key_row_block = kv_block[0].reshape(kv_block.shape[1], kv_heads, HEAD_SIZE)
        value_row_block = kv_block[1].reshape(kv_block.shape[1], kv_heads, HEAD_SIZE)
        scores = (
            jnp.einsum("tgrd,ugd->grtu", grouped, key_row_block, preferred_element_type=jnp.float32)
            * score_scale
        )
        new_max = jnp.maximum(running_max, jnp.max(scores, axis=-1))
        rescale = jnp.exp(running_max - new_max)
        weights = jnp.exp(scores - new_max[..., None])
        row_total = row_total * rescale + jnp.sum(weights, axis=-1)
        added = jnp.einsum(
            "grtu,ugd->grtd",
            weights.astype(jnp.bfloat16),
            value_row_block,
            preferred_element_type=jnp.float32,
        )
        weighted = weighted * rescale[..., None] + added
        return (new_max, row_total, weighted)

    def keep_state(carry_state):
        return carry_state

    initial = (
        jnp.full((kv_heads, query_group_size, span_len), -1e30, jnp.float32),
        jnp.zeros((kv_heads, query_group_size, span_len), jnp.float32),
        jnp.zeros((kv_heads, query_group_size, span_len, HEAD_SIZE), jnp.float32),
    )
    final_state = update(initial, kv_pair)
    moving = kv_pair
    for distance in range(1, OLDER_SPAN_LIMIT + 1):
        moving = shifted(moving, "span", 1)
        guarded_kv_block = moving
        visible = (distance >= 0) & (distance <= older_mine)
        final_state = lax.cond(
            visible, lambda current: update(current, guarded_kv_block), keep_state, final_state
        )
    running_max, row_total, weighted = final_state
    attention = (weighted / row_total[..., None]).astype(jnp.bfloat16)
    attention = attention.transpose(2, 0, 1, 3).reshape(span_len, q_heads * HEAD_SIZE)
    projected = lax.psum_scatter(
        jnp.dot(attention, out_weight, preferred_element_type=jnp.float32).astype(jnp.bfloat16),
        "head",
        scatter_dimension=0,
        tiled=True,
    ).astype(jnp.float32)
    step_mine = noise_step[my_span]
    one_hot = (jnp.arange(gate_table.shape[0], dtype=jnp.int32) == step_mine).astype(jnp.float32)
    gate_row = jnp.dot(one_hot[None, :], gate_table, precision=lax.Precision.HIGHEST)
    return (residual.astype(jnp.float32) + gate_row * projected).astype(jnp.bfloat16)


def solution(mesh):
    in_specs = (
        P("span", "head"),
        P("span", "head"),
        P("span", "head"),
        P("head", None),
        P(("span", "head"), None),
        P(),
        P(),
        P(),
    )
    out_specs = P(("span", "head"), None)
    return jax.shard_map(
        on_device, mesh=mesh, in_specs=in_specs, out_specs=out_specs, check_vma=False
    )
```

profile of v0, /device:TPU:17, one launch (start us, length us, event | category | flops | bytes accessed | tf_op | source)
XLA Modules:
  0.0 527.2 jit_solution(6040263411048018499)
XLA Ops:
  13.0 11.7 %collective-permute-done = bf16[2,512,512]{1,2,0:T(8,128)(2,1)S(1)} collective-permute-done((bf16[2,512,512]{1,2,0:T(8,128)(2,1)S(1)}, bf16[2,512,512]{1,2,0:T(8,128)(2,1)S(1)}, u32[]{:S(2)}, u32[]{:S(2)}) %collective-permute-start) | collective-permute-done | bytes 1048608 | tf_op jit(solution)/shard_map/ppermute | solution.py:15
  29.1 11.7 %collective-permute-done.1 = bf16[2,512,512]{1,2,0:T(8,128)(2,1)S(1)} collective-permute-done((bf16[2,512,512]{1,2,0:T(8,128)(2,1)S(1)}, bf16[2,512,512]{1,2,0:T(8,128)(2,1)S(1)}, u32[]{:S(2)}, u32[]{:S(2)}) %collective-permute-start.1) | collective-permute-done | bytes 1048608 | tf_op jit(solution)/shard_map/ppermute | solution.py:15
  45.2 11.7 %collective-permute-done.2 = bf16[2,512,512]{1,2,0:T(8,128)(2,1)} collective-permute-done((bf16[2,512,512]{1,2,0:T(8,128)(2,1)S(1)}, bf16[2,512,512]{1,2,0:T(8,128)(2,1)}, u32[]{:S(2)}, u32[]{:S(2)}) %collective-permute-start.2) | collective-permute-done | bytes 1048608 | tf_op jit(solution)/shard_map/ppermute | solution.py:15
  77.7 12.0 %bitcast_reduce_fusion.7 = (f32[4,6,512]{2,1,0:T(8,128)S(1)}, f32[4,512,512,6]{2,1,3,0:T(8,128)}) fusion(bf16[512,4,6,128]{0,3,2,1:T(8,128)(2,1)} %bitcast.211, bf16[512,4,128,1]{2,1,0,3:T(4,128)(2,1)S(1)} %bitcast.221), kind=kOutput, calls=%fused_computation.85 | convolution fusion | flops 1623183360 | bytes 28884992 | tf_op jit(solution)/shard_map/tgrd,ugd->grtu/dot_general | solution.py:43
  110.3 13.2 %broadcast_add_fusion = f32[4,6,512,128]{3,2,1,0:T(8,128)} fusion(f32[4,6,512]{2,1,0:T(8,128)S(1)} %get-tuple-element.270, f32[4,512,512,6]{2,1,3,0:T(8,128)} %get-tuple-element.273, f32[4,6,512]{2,1,0:T(8,128)S(1)} %broadcast_maximum_fusion, bf16[512,4,128,1]{2,1,0,3:T(4,128)(2,1)S(1)} %bitcast.220), kind=kOutput, calls=%fused_computation.95 | convolution fusion | flops 1631059968 | bytes 32079872 | tf_op jit(solution)/shard_map/grtu,ugd->grtd/dot_general | solution.py:50
  123.5 39.2 %conditional.7 = ((f32[4,6,512]{2,1,0:T(8,128)S(1)}, f32[4,6,512]{2,1,0:T(8,128)S(1)}, f32[4,6,512,128]{3,2,1,0:T(8,128)})) conditional(s32[]{:T(128)} %bitcast.44, (f32[4,6,512]{2,1,0:T(8,128)S(1)}, f32[4,6,512]{2,1,0:T(8,128)S(1)}, f32[4,6,512,128]{3,2,1,0:T(8,128)}) %tuple.49, (bf16[2,512,512]{1,2,0:T(8,128)(2,1)}, ...), branch_computations={%region_2.0_spmd, %region_3.0_spmd} | conditional | flops 3274727424 | bytes 95158304 | solution.py:73
  125.0 12.0 %bitcast_reduce_fusion = (f32[4,6,512]{2,1,0:T(8,128)S(1)}, f32[4,512,512,6]{2,1,3,0:T(8,128)}) fusion(bf16[512,4,128,1]{0,2,3,1:T(8,128)(2,1)S(1)} %bitcast.229, bf16[512,4,6,128]{0,3,2,1:T(8,128)(2,1)} %get-tuple-element.191), kind=kOutput, calls=%fused_computation.1 | convolution fusion | flops 1623183360 | bytes 28884992 | tf_op jit(solution)/shard_map/cond/branch_1_fun/tgrd,ugd->grtu/dot_general | solution.py:43
  147.5 15.2 %multiply_add_fusion = f32[4,6,512,128]{3,2,1,0:T(8,128)} fusion(f32[4,6,512,128]{3,2,1,0:T(8,128)} %get-tuple-element.119, f32[4,6,512]{2,1,0:T(8,128)S(1)} %get-tuple-element.229, bf16[512,4,128,1]{0,2,3,1:T(8,128)(2,1)S(1)} %bitcast.222, f32[4,512,512,6]{2,1,3,0:T(8,128)} %get-tuple-element.245, f32[4,6,512]{2,1,0:T(8,128)S(1)} %max.14), kind=kOutput, calls=%fused_computation.8 | convolution fusion | flops 1632632832 | bytes 38371328 | tf_op jit(solution)/shard_map/cond/branch_1_fun/grtu,ugd->grtd/dot_general | solution.py:50
  162.7 39.2 %conditional.8 = ((f32[4,6,512]{2,1,0:T(8,128)S(1)}, f32[4,6,512]{2,1,0:T(8,128)S(1)}, f32[4,6,512,128]{3,2,1,0:T(8,128)})) conditional(s32[]{:T(128)} %bitcast.43, (f32[4,6,512]{2,1,0:T(8,128)S(1)}, f32[4,6,512]{2,1,0:T(8,128)S(1)}, f32[4,6,512,128]{3,2,1,0:T(8,128)}) %get-tuple-element.314, (bf16[2,512,512]{1,2,0:T(8,128)(2,1)}, ...), branch_computations={%region_6.0_spmd, %region_7.0_spmd} | conditional | flops 3274727424 | bytes 95158304 | solution.py:73
  164.2 12.0 %bitcast_reduce_fusion.1 = (f32[4,6,512]{2,1,0:T(8,128)S(1)}, f32[4,512,512,6]{2,1,3,0:T(8,128)}) fusion(bf16[512,4,128,1]{0,2,3,1:T(8,128)(2,1)S(1)} %bitcast.230, bf16[512,4,6,128]{0,3,2,1:T(8,128)(2,1)} %get-tuple-element.196), kind=kOutput, calls=%fused_computation.13 | convolution fusion | flops 1623183360 | bytes 28884992 | tf_op jit(solution)/shard_map/cond/branch_1_fun/tgrd,ugd->grtu/dot_general | solution.py:43
  176.2 10.5 %fusion.12 = f32[4,6,512]{2,1,0:T(8,128)S(1)} fusion(f32[4,512,512,6]{2,1,3,0:T(8,128)} %get-tuple-element.249, f32[4,6,512]{2,1,0:T(8,128)S(1)} %max.15), kind=kLoop, calls=%fused_computation.16 | loop fusion | flops 18862080 | bytes 25264128 | tf_op jit(solution)/shard_map/cond/branch_1_fun/reduce_sum | solution.py:49
  186.7 15.2 %multiply_add_fusion.2 = f32[4,6,512,128]{3,2,1,0:T(8,128)} fusion(f32[4,6,512,128]{3,2,1,0:T(8,128)} %get-tuple-element.124, f32[4,6,512]{2,1,0:T(8,128)S(1)} %get-tuple-element.231, bf16[512,4,128,1]{0,2,3,1:T(8,128)(2,1)S(1)} %bitcast.223, f32[4,512,512,6]{2,1,3,0:T(8,128)} %get-tuple-element.249, f32[4,6,512]{2,1,0:T(8,128)S(1)} %max.15), kind=kOutput, calls=%fused_computation.20 | convolution fusion | flops 1632632832 | bytes 38371328 | tf_op jit(solution)/shard_map/cond/branch_1_fun/grtu,ugd->grtd/dot_general | solution.py:50
  201.9 39.3 %conditional.9 = ((f32[4,6,512]{2,1,0:T(8,128)S(1)}, f32[4,6,512]{2,1,0:T(8,128)S(1)}, f32[4,6,512,128]{3,2,1,0:T(8,128)})) conditional(s32[]{:T(128)} %bitcast.42, (f32[4,6,512]{2,1,0:T(8,128)S(1)}, f32[4,6,512]{2,1,0:T(8,128)S(1)}, f32[4,6,512,128]{3,2,1,0:T(8,128)}) %get-tuple-element.315, (bf16[2,512,512]{1,2,0:T(8,128)(2,1)}, ...), branch_computations={%region_10.0_spmd, %region_11.0_spmd} | conditional | flops 3274727424 | bytes 95158304 | solution.py:73
  203.5 12.0 %bitcast_reduce_fusion.2 = (f32[4,6,512]{2,1,0:T(8,128)S(1)}, f32[4,512,512,6]{2,1,3,0:T(8,128)}) fusion(bf16[512,4,128,1]{0,2,3,1:T(8,128)(2,1)S(1)} %bitcast.231, bf16[512,4,6,128]{0,3,2,1:T(8,128)(2,1)} %get-tuple-element.201), kind=kOutput, calls=%fused_computation.25 | convolution fusion | flops 1623183360 | bytes 28884992 | tf_op jit(solution)/shard_map/cond/branch_1_fun/tgrd,ugd->grtu/dot_general | solution.py:43
  226.0 15.2 %multiply_add_fusion.4 = f32[4,6,512,128]{3,2,1,0:T(8,128)} fusion(f32[4,6,512,128]{3,2,1,0:T(8,128)} %get-tuple-element.129, f32[4,6,512]{2,1,0:T(8,128)S(1)} %get-tuple-element.233, bf16[512,4,128,1]{0,2,3,1:T(8,128)(2,1)S(1)} %bitcast.224, f32[4,512,512,6]{2,1,3,0:T(8,128)} %get-tuple-element.253, f32[4,6,512]{2,1,0:T(8,128)S(1)} %max.16), kind=kOutput, calls=%fused_computation.32 | convolution fusion | flops 1632632832 | bytes 38371328 | tf_op jit(solution)/shard_map/cond/branch_1_fun/grtu,ugd->grtd/dot_general | solution.py:50
  241.2 38.3 %conditional.10 = ((f32[4,6,512]{2,1,0:T(8,128)S(1)}, f32[4,6,512]{2,1,0:T(8,128)S(1)}, f32[4,6,512,128]{3,2,1,0:T(8,128)})) conditional(s32[]{:T(128)} %bitcast.41, (f32[4,6,512]{2,1,0:T(8,128)S(1)}, f32[4,6,512]{2,1,0:T(8,128)S(1)}, f32[4,6,512,128]{3,2,1,0:T(8,128)}) %get-tuple-element.316, (bf16[2,512,512]{1,2,0:T(8,128)(2,1)S(1)}, ...), branch_computations={%region_14.0_spmd, %region_15.0_spmd} | conditional | flops 3274727424 | bytes 95158304 | solution.py:73
  241.8 12.0 %bitcast_reduce_fusion.3 = (f32[4,6,512]{2,1,0:T(8,128)S(1)}, f32[4,512,512,6]{2,1,3,0:T(8,128)}) fusion(bf16[512,4,128,1]{0,2,3,1:T(8,128)(2,1)S(1)} %bitcast.232, bf16[512,4,6,128]{0,3,2,1:T(8,128)(2,1)} %get-tuple-element.206), kind=kOutput, calls=%fused_computation.37 | convolution fusion | flops 1623183360 | bytes 28884992 | tf_op jit(solution)/shard_map/cond/branch_1_fun/tgrd,ugd->grtu/dot_general | solution.py:43
  253.8 10.5 %fusion.32 = f32[4,6,512]{2,1,0:T(8,128)S(1)} fusion(f32[4,512,512,6]{2,1,3,0:T(8,128)} %get-tuple-element.257, f32[4,6,512]{2,1,0:T(8,128)S(1)} %max.17), kind=kLoop, calls=%fused_computation.40 | loop fusion | flops 18862080 | bytes 25264128 | tf_op jit(solution)/shard_map/cond/branch_1_fun/reduce_sum | solution.py:49
  264.4 15.2 %multiply_add_fusion.6 = f32[4,6,512,128]{3,2,1,0:T(8,128)} fusion(f32[4,6,512,128]{3,2,1,0:T(8,128)} %get-tuple-element.134, f32[4,6,512]{2,1,0:T(8,128)S(1)} %get-tuple-element.235, bf16[512,4,128,1]{0,2,3,1:T(8,128)(2,1)S(1)} %bitcast.225, f32[4,512,512,6]{2,1,3,0:T(8,128)} %get-tuple-element.257, f32[4,6,512]{2,1,0:T(8,128)S(1)} %max.17), kind=kOutput, calls=%fused_computation.44 | convolution fusion | flops 1632632832 | bytes 38371328 | tf_op jit(solution)/shard_map/cond/branch_1_fun/grtu,ugd->grtd/dot_general | solution.py:50
  279.5 39.2 %conditional.11 = ((f32[4,6,512]{2,1,0:T(8,128)S(1)}, f32[4,6,512]{2,1,0:T(8,128)S(1)}, f32[4,6,512,128]{3,2,1,0:T(8,128)})) conditional(s32[]{:T(128)} %bitcast.40, (f32[4,6,512]{2,1,0:T(8,128)S(1)}, f32[4,6,512]{2,1,0:T(8,128)S(1)}, f32[4,6,512,128]{3,2,1,0:T(8,128)}) %get-tuple-element.317, (bf16[2,512,512]{1,2,0:T(8,128)(2,1)}, ...), branch_computations={%region_18.0_spmd, %region_19.0_spmd} | conditional | flops 3274727424 | bytes 95158304 | solution.py:73
  281.0 12.0 %bitcast_reduce_fusion.4 = (f32[4,6,512]{2,1,0:T(8,128)S(1)}, f32[4,512,512,6]{2,1,3,0:T(8,128)}) fusion(bf16[512,4,128,1]{0,2,3,1:T(8,128)(2,1)S(1)} %bitcast.233, bf16[512,4,6,128]{0,3,2,1:T(8,128)(2,1)} %get-tuple-element.211), kind=kOutput, calls=%fused_computation.49 | convolution fusion | flops 1623183360 | bytes 28884992 | tf_op jit(solution)/shard_map/cond/branch_1_fun/tgrd,ugd->grtu/dot_general | solution.py:43
  293.0 10.5 %fusion.42 = f32[4,6,512]{2,1,0:T(8,128)S(1)} fusion(f32[4,512,512,6]{2,1,3,0:T(8,128)} %get-tuple-element.261, f32[4,6,512]{2,1,0:T(8,128)S(1)} %max.18), kind=kLoop, calls=%fused_computation.52 | loop fusion | flops 18862080 | bytes 25264128 | tf_op jit(solution)/shard_map/cond/branch_1_fun/reduce_sum | solution.py:49
  303.5 15.2 %multiply_add_fusion.8 = f32[4,6,512,128]{3,2,1,0:T(8,128)} fusion(f32[4,6,512,128]{3,2,1,0:T(8,128)} %get-tuple-element.139, f32[4,6,512]{2,1,0:T(8,128)S(1)} %get-tuple-element.237, bf16[512,4,128,1]{0,2,3,1:T(8,128)(2,1)S(1)} %bitcast.226, f32[4,512,512,6]{2,1,3,0:T(8,128)} %get-tuple-element.261, f32[4,6,512]{2,1,0:T(8,128)S(1)} %max.18), kind=kOutput, calls=%fused_computation.56 | convolution fusion | flops 1632632832 | bytes 38371328 | tf_op jit(solution)/shard_map/cond/branch_1_fun/grtu,ugd->grtd/dot_general | solution.py:50
  318.7 39.2 %conditional.12 = ((f32[4,6,512]{2,1,0:T(8,128)S(1)}, f32[4,6,512]{2,1,0:T(8,128)S(1)}, f32[4,6,512,128]{3,2,1,0:T(8,128)})) conditional(s32[]{:T(128)} %bitcast.39, (f32[4,6,512]{2,1,0:T(8,128)S(1)}, f32[4,6,512]{2,1,0:T(8,128)S(1)}, f32[4,6,512,128]{3,2,1,0:T(8,128)}) %get-tuple-element.318, (bf16[2,512,512]{1,2,0:T(8,128)(2,1)}, ...), branch_computations={%region_22.0_spmd, %region_23.0_spmd} | conditional | flops 3274727424 | bytes 95158304 | solution.py:73
  320.2 12.0 %bitcast_reduce_fusion.5 = (f32[4,6,512]{2,1,0:T(8,128)S(1)}, f32[4,512,512,6]{2,1,3,0:T(8,128)}) fusion(bf16[512,4,128,1]{0,2,3,1:T(8,128)(2,1)S(1)} %bitcast.234, bf16[512,4,6,128]{0,3,2,1:T(8,128)(2,1)} %get-tuple-element.216), kind=kOutput, calls=%fused_computation.61 | convolution fusion | flops 1623183360 | bytes 28884992 | tf_op jit(solution)/shard_map/cond/branch_1_fun/tgrd,ugd->grtu/dot_general | solution.py:43
  332.2 10.5 %fusion.52 = f32[4,6,512]{2,1,0:T(8,128)S(1)} fusion(f32[4,512,512,6]{2,1,3,0:T(8,128)} %get-tuple-element.265, f32[4,6,512]{2,1,0:T(8,128)S(1)} %max.19), kind=kLoop, calls=%fused_computation.64 | loop fusion | flops 18862080 | bytes 25264128 | tf_op jit(solution)/shard_map/cond/branch_1_fun/reduce_sum | solution.py:49
  342.7 15.2 %multiply_add_fusion.10 = f32[4,6,512,128]{3,2,1,0:T(8,128)} fusion(f32[4,6,512,128]{3,2,1,0:T(8,128)} %get-tuple-element.144, f32[4,6,512]{2,1,0:T(8,128)S(1)} %get-tuple-element.239, bf16[512,4,128,1]{0,2,3,1:T(8,128)(2,1)S(1)} %bitcast.227, f32[4,512,512,6]{2,1,3,0:T(8,128)} %get-tuple-element.265, f32[4,6,512]{2,1,0:T(8,128)S(1)} %max.19), kind=kOutput, calls=%fused_computation.68 | convolution fusion | flops 1632632832 | bytes 38371328 | tf_op jit(solution)/shard_map/cond/branch_1_fun/grtu,ugd->grtd/dot_general | solution.py:50
  357.9 46.1 %conditional.13 = (f32[4,6,512]{2,1,0:T(8,128)S(1)}, f32[4,6,512,128]{2,3,1,0:T(8,128)}) conditional(s32[]{:T(128)} %bitcast.38, (f32[4,6,512]{2,1,0:T(8,128)S(1)}, f32[4,6,512,128]{3,2,1,0:T(8,128)}) %tuple.56, (bf16[2,512,512]{1,2,0:T(8,128)(2,1)}, bf16[512,4,6,128]{0,3,2,1:T(8,128)(2,1)}, f32[4,6,512]{2,1,0:T(8,128)S(1)}, ...), branch_computations={%region_26.0_spmd, %region_27.0_spmd} | conditional | flops 3274727424 | bytes 107642896 | solution.py:73
  359.5 12.0 %bitcast_reduce_fusion.6 = (f32[4,6,512]{2,1,0:T(8,128)S(1)}, f32[4,512,512,6]{2,1,3,0:T(8,128)}) fusion(bf16[512,4,128,1]{0,2,3,1:T(8,128)(2,1)S(1)} %bitcast.235, bf16[512,4,6,128]{0,3,2,1:T(8,128)(2,1)} %get-tuple-element.221), kind=kOutput, calls=%fused_computation.73 | convolution fusion | flops 1623183360 | bytes 28884992 | tf_op jit(solution)/shard_map/cond/branch_1_fun/tgrd,ugd->grtu/dot_general | solution.py:43
  382.0 15.2 %multiply_add_fusion.12 = f32[4,6,512,128]{3,2,1,0:T(8,128)} fusion(f32[4,6,512,128]{3,2,1,0:T(8,128)} %get-tuple-element.149, f32[4,6,512]{2,1,0:T(8,128)S(1)} %get-tuple-element.241, bf16[512,4,128,1]{0,2,3,1:T(8,128)(2,1)S(1)} %bitcast.228, f32[4,512,512,6]{2,1,3,0:T(8,128)} %get-tuple-element.269, f32[4,6,512]{2,1,0:T(8,128)S(1)} %max.20), kind=kOutput, calls=%fused_computation.80 | convolution fusion | flops 1632632832 | bytes 38371328 | tf_op jit(solution)/shard_map/cond/branch_1_fun/grtu,ugd->grtd/dot_general | solution.py:50
  407.7 26.7 %convolution_convert_fusion = bf16[512,6144]{1,0:T(8,128)(2,1)} fusion(bf16[512,3072]{0,1:T(8,128)(2,1)S(1)} %bitcast.219, bf16[3072,6144]{1,0:T(8,128)(2,1)} %param.25), kind=kOutput, calls=%fused_computation.92 | convolution fusion | flops 19330498560 | bytes 47185920 | tf_op jit(solution)/shard_map/dot_general | solution.py:80
  436.1 78.0 %reduce-scatter.2.cloned.1.call-done = bf16[256,6144]{1,0:T(8,128)(2,1)} async-done(((bf16[512,6144]{1,0:T(8,128)(2,1)}), bf16[256,6144]{1,0:T(8,128)(2,1)}) %reduce-scatter.2.cloned.1.call-update) | async-done | bytes 3145744 | tf_op jit(solution)/shard_map/reduce_scatter | solution.py:79
  (68 shorter events, 109.3 us)
Async XLA Ops:
  6.5 428.6 %copy-start = (f32[32,6144]{1,0:T(8,128)S(1)}, f32[32,6144]{1,0:T(8,128)}, u32[]{:S(2)}) copy-start(f32[32,6144]{1,0:T(8,128)} %param.27) | copy-start | bytes 2359300
  6.5 507.6 %reduce-scatter.2.cloned.1.call-start = ((), (), s32[]{:S(2)}) async-start(), calls=%async_computation.1 | async-start | bytes 9437184 | tf_op jit(solution)/shard_map/reduce_scatter | solution.py:79
  9.2 15.4 %collective-permute-start = (bf16[2,512,512]{1,2,0:T(8,128)(2,1)S(1)}, bf16[2,512,512]{1,2,0:T(8,128)(2,1)S(1)}, u32[]{:S(2)}, u32[]{:S(2)}) collective-permute-start(bf16[2,512,512]{1,2,0:T(8,128)(2,1)S(1)} %pad_maximum_fusion), channel_id=1, source_target_pairs={{0,2},{2,4},{4,6},{6,8},{8,10},{10,12},{12,14},{14,16},{16,18},{18... | collective-permute-start | bytes 3145736 | tf_op jit(solution)/shard_map/ppermute | solution.py:15
  24.7 32.2 %copy-start.3 = (bf16[2,512,512]{1,2,0:T(8,128)(2,1)}, bf16[2,512,512]{1,2,0:T(8,128)(2,1)S(1)}, u32[]{:S(2)}) copy-start(bf16[2,512,512]{1,2,0:T(8,128)(2,1)S(1)} %collective-permute-done) | copy-start | bytes 3145732
  24.7 16.1 %collective-permute-start.1 = (bf16[2,512,512]{1,2,0:T(8,128)(2,1)S(1)}, bf16[2,512,512]{1,2,0:T(8,128)(2,1)S(1)}, u32[]{:S(2)}, u32[]{:S(2)}) collective-permute-start(bf16[2,512,512]{1,2,0:T(8,128)(2,1)S(1)} %collective-permute-done), channel_id=1, source_target_pairs={{0,2},{2,4},{4,6},{6,8},{8,10},{10,12},{12,14},{14,16},{16,18},{18... | collective-permute-start | bytes 3145736 | tf_op jit(solution)/shard_map/ppermute | solution.py:15
  40.8 16.1 %copy-start.2 = (bf16[2,512,512]{1,2,0:T(8,128)(2,1)}, bf16[2,512,512]{1,2,0:T(8,128)(2,1)S(1)}, u32[]{:S(2)}) copy-start(bf16[2,512,512]{1,2,0:T(8,128)(2,1)S(1)} %collective-permute-done.1) | copy-start | bytes 3145732
  40.8 16.1 %collective-permute-start.2 = (bf16[2,512,512]{1,2,0:T(8,128)(2,1)S(1)}, bf16[2,512,512]{1,2,0:T(8,128)(2,1)}, u32[]{:S(2)}, u32[]{:S(2)}) collective-permute-start(bf16[2,512,512]{1,2,0:T(8,128)(2,1)S(1)} %collective-permute-done.1), channel_id=1, source_target_pairs={{0,2},{2,4},{4,6},{6,8},{8,10},{10,12},{12,14},{14,16},{16,18},{18... | collective-permute-start | bytes 3145736 | tf_op jit(solution)/shard_map/ppermute | solution.py:15
  56.9 17.0 %collective-permute-start.3 = (bf16[2,512,512]{1,2,0:T(8,128)(2,1)}, bf16[2,512,512]{1,2,0:T(8,128)(2,1)S(1)}, u32[]{:S(2)}, u32[]{:S(2)}) collective-permute-start(bf16[2,512,512]{1,2,0:T(8,128)(2,1)} %collective-permute-done.2), channel_id=1, source_target_pairs={{0,2},{2,4},{4,6},{6,8},{8,10},{10,12},{12,14},{14,16},{16,18},{18... | collective-permute-start | bytes 3145736 | tf_op jit(solution)/shard_map/ppermute | solution.py:15
  73.9 15.8 %collective-permute-start.4 = (bf16[2,512,512]{1,2,0:T(8,128)(2,1)S(1)}, bf16[2,512,512]{1,2,0:T(8,128)(2,1)S(1)}, u32[]{:S(2)}, u32[]{:S(2)}) collective-permute-start(bf16[2,512,512]{1,2,0:T(8,128)(2,1)S(1)} %collective-permute-done.3), channel_id=1, source_target_pairs={{0,2},{2,4},{4,6},{6,8},{8,10},{10,12},{12,14},{14,16},{16,18},{18... | collective-permute-start | bytes 3145736 | tf_op jit(solution)/shard_map/ppermute | solution.py:15
  89.7 4.4 copy-start.1
  89.7 16.1 %collective-permute-start.5 = (bf16[2,512,512]{1,2,0:T(8,128)(2,1)S(1)}, bf16[2,512,512]{1,2,0:T(8,128)(2,1)}, u32[]{:S(2)}, u32[]{:S(2)}) collective-permute-start(bf16[2,512,512]{1,2,0:T(8,128)(2,1)S(1)} %collective-permute-done.4), channel_id=1, source_target_pairs={{0,2},{2,4},{4,6},{6,8},{8,10},{10,12},{12,14},{14,16},{16,18},{18... | collective-permute-start | bytes 3145736 | tf_op jit(solution)/shard_map/ppermute | solution.py:15
  105.8 252.1 %collective-permute-start.6 = (bf16[2,512,512]{1,2,0:T(8,128)(2,1)}, bf16[2,512,512]{1,2,0:T(8,128)(2,1)}, u32[]{:S(2)}, u32[]{:S(2)}) collective-permute-start(bf16[2,512,512]{1,2,0:T(8,128)(2,1)} %collective-permute-done.5), channel_id=1, source_target_pairs={{0,2},{2,4},{4,6},{6,8},{8,10},{10,12},{12,14},{14,16},{16,18},{18... | collective-permute-start | bytes 3145736 | tf_op jit(solution)/shard_map/ppermute | solution.py:15
  407.7 26.8 %copy-start.4 = (s32[16]{0:T(128)S(1)}, s32[16]{0:T(128)}, u32[]{:S(2)}) copy-start(s32[16]{0:T(128)} %param.28) | copy-start | bytes 196
Sparse Core Ops, SparseCore 0:
  434.6 79.4 reduce-scatter.1
where the time goes:
time: 537 us; the launch traced here: 527 us
  matrix products  243 us (45%)
  waiting for transfers between devices  114 us (21%)
  other arithmetic  93.7 us (17%)
  starting transfers between devices  29.6 us (6%)
  local copies, waits for them, and re-layouts  25.7 us (5%)
  between operations  18.4 us (3%)
    dot_general x8, matrix products, update(): jnp.einsum('grtu,ugd->grtd', weights.astype(jnp.bfloat16), value_row_bloc...  119 us
    dot_general x8, matrix products, update(): jnp.einsum('tgrd,ugd->grtu', grouped, key_row_block, preferred_element_ty...  95.9 us
    reduce_sum x8, other arithmetic, update(): row_total = row_total * rescale + jnp.sum(weights, axis=-1)  83.8 us
    reduce_scatter x1, waiting for transfers between devices, on_device(): lax.psum_scatter(jnp.dot(attention, out_weight, preferred_element_type=jn...  78 us
    ppermute x7, waiting for transfers between devices, shifted(): return lax.ppermute(block, axis, route)  36.4 us
    ppermute x7, starting transfers between devices, shifted(): return lax.ppermute(block, axis, route)  29.6 us
    dot_general x1, matrix products, on_device(): jnp.dot(attention, out_weight, preferred_element_type=jnp.float32)  26.7 us
  transfers between devices with their start and end apart: 8, of which 5 were waited for; matrix products, arithmetic and copies ran while one was open for 53% of the time, Pallas kernels for 0%

commit v1 on v0

v1 whole, which is shorter than its diff:
```python
import functools
import math

import jax
import jax.numpy as jnp
from jax import lax
from jax.experimental import pallas as pl
from jax.experimental.pallas import tpu as pltpu
from jax.sharding import PartitionSpec as P

HEAD_SIZE = 128
MAX_BLOCKS = 8
EXPONENT_SCALE = math.log2(math.e) / math.sqrt(HEAD_SIZE)
TOTAL_LIMIT = 2.0**100
F32 = jnp.float32
BF16 = jnp.bfloat16
NT = (((1,), (1,)), ((), ()))


def slot_source(slot, my_span):
    core, y = my_span & 1, (my_span >> 1) & 1
    plane = my_span - 4
    return [
        (my_span, y >= 0),
        (my_span ^ 1, core == 1),
        (my_span ^ 2, y == 1),
        (my_span ^ 3, y == 1),
        (plane, y >= 0),
        (plane ^ 1, y >= 0),
        (plane ^ 2, y == 0),
        (plane ^ 3, y == 0),
        (plane ^ 2, y == 1),
        (plane ^ 3, y == 1),
        (my_span - 7, core == 0),
        (my_span - 6, y == 0),
        ((my_span - 6) ^ 1, y == 0),
    ][slot]


def attention_kernel(slots, rows, group, sub, first, last, place, older_count, q_ref, *rest):
    kv_refs, rest = rest[: len(slots)], rest[len(slots) :]
    if not first:
        (sum_in, mark_in), rest = rest[:2], rest[2:]
    if last:
        weight_ref, out_ref, product_ref, keys, values, scaled, acc, mark, attended, near_weight, arrived = rest
        load = pltpu.make_async_copy(weight_ref.at[:, pl.ds(0, near_weight.shape[1])], near_weight, arrived)
        pl.when(pl.program_id(0) == 0)(load.start)
    else:
        sum_out, mark, keys, values, scaled, acc = rest
    half = HEAD_SIZE // 2
    span = kv_refs[0].shape[1]
    my_span = place[1]
    older_mine = older_count[my_span]

    def pack(at, j):
        key_block = kv_refs[j][0]
        keys[at, :, :HEAD_SIZE] = key_block
        keys[at, :, HEAD_SIZE:] = key_block
        values[at, :, :HEAD_SIZE] = kv_refs[j][1]
        values[at, :, HEAD_SIZE:] = jnp.ones((span, HEAD_SIZE), BF16)

    count = jnp.int32(0)
    for j, slot in enumerate(slots):
        if slot == 0:
            pack(0, 0)
            count = jnp.int32(1)
        else:
            source, used = slot_source(slot, my_span)
            seen = used & (source < my_span) & (my_span - source <= older_mine)
            pl.when(seen)(functools.partial(pack, count, j))
            count = count + jnp.where(seen, 1, 0).astype(jnp.int32)

    def scale():
        for h in range(group):
            q = q_ref[:, h * HEAD_SIZE : (h + 1) * HEAD_SIZE].astype(F32) * EXPONENT_SCALE
            high = q.astype(BF16)
            scaled[h * rows : (h + 1) * rows, :HEAD_SIZE] = high
            scaled[h * rows : (h + 1) * rows, HEAD_SIZE:] = (q - high.astype(F32)).astype(BF16)

    n_sub = group * rows // sub

    def scores(at, block):
        return lax.dot_general(scaled[at, :], keys[block], NT, preferred_element_type=F32)

    def weigh(p, block):
        return jnp.dot(p.astype(BF16), values[block], preferred_element_type=F32)

    if first:
        scale()
        mark[:, :half] = jnp.zeros((group * rows, half), F32)
        for i in range(n_sub):
            at = pl.ds(i * sub, sub)
            s = scores(at, 0)
            row_top = jnp.max(s, axis=1, keepdims=True)
            mark[at, half:] = jnp.broadcast_to(row_top, (sub, half))
            acc[at, :] = weigh(jnp.exp2(s - row_top), 0)
    else:
        pl.when(count > 0)(scale)
        acc[:, :HEAD_SIZE] = sum_in[...]
        acc[:, HEAD_SIZE:] = jnp.zeros((group * rows, HEAD_SIZE), F32)
        mark[...] = mark_in[...]

    def add_block(block):
        for i in range(n_sub):
            at = pl.ds(i * sub, sub)
            acc[at, :] += weigh(jnp.exp2(scores(at, block) - mark[at, half : half + 1]), block)

    begin = 1 if first else 0
    if len(slots) > begin:
        pairs = (count - begin) // 2

        def two_blocks(i, carry):
            add_block(begin + 2 * i)
            add_block(begin + 2 * i + 1)
            return carry

        lax.fori_loop(0, pairs, two_blocks, 0)
        pl.when(begin + 2 * pairs < count)(functools.partial(add_block, count - 1))

        @pl.when(jnp.logical_not(jnp.max(acc[:, HEAD_SIZE:]) < TOTAL_LIMIT))
        def _():
            def again(i, carry):
                at = pl.ds(pl.multiple_of(i * sub, sub), sub)
                acc[at, :] = jnp.zeros((sub, 2 * HEAD_SIZE), F32)
                if first:
                    mark[at, half:] = jnp.full((sub, half), -1e30, F32)
                else:
                    acc[at, :HEAD_SIZE] = sum_in[at, :]
                    mark[at, :] = mark_in[at, :]

                def block_step(block, inner):
                    s = scores(at, block)
                    old_top = mark[at, half : half + 1]
                    new_top = jnp.maximum(old_top, jnp.max(s, axis=1, keepdims=True))
                    shrink = jnp.exp2(old_top - new_top)
                    mark[at, :half] = mark[at, :half] * shrink
                    mark[at, half:] = jnp.broadcast_to(new_top, (sub, half))
                    acc[at, :] = acc[at, :] * shrink + weigh(jnp.exp2(s - new_top), block)
                    return inner

                return lax.fori_loop(0, count, block_step, carry)

            lax.fori_loop(0, n_sub, again, 0)

    if not last:
        mark[:, :half] += acc[:, HEAD_SIZE : HEAD_SIZE + half]
        sum_out[...] = acc[:, :HEAD_SIZE]
        return
    head = pl.program_id(0)
    for h in range(group):
        at = pl.ds(h * rows, rows)
        total = acc[at, HEAD_SIZE:] + mark[at, :1]
        result = (acc[at, :HEAD_SIZE] / total).astype(BF16)
        out_ref[:, h * HEAD_SIZE : (h + 1) * HEAD_SIZE] = result
        here = (head * group + h) * HEAD_SIZE
        attended[:, pl.ds(pl.multiple_of(here, HEAD_SIZE), HEAD_SIZE)] = result

    @pl.when(head == pl.num_programs(0) - 1)
    def _():
        load.wait()
        tile = 512
        for begin in range(0, product_ref.shape[1], tile):
            at = slice(begin, begin + tile)
            product = jnp.dot(attended[...], near_weight[:, at], preferred_element_type=F32)
            product_ref[:, at] = product.astype(BF16)


def attention(queries, place, older_count, rows, group, blocks, state=None, weight=None, columns=0):
    slots = sorted(blocks)
    arrays = [blocks[slot] for slot in slots]
    first = state is None
    last = weight is not None
    kv_heads = arrays[0].shape[2] // HEAD_SIZE
    span = arrays[0].shape[1]
    width = group * HEAD_SIZE
    all_rows = group * rows
    n_block = min(MAX_BLOCKS, len(arrays))
    state_spec = pl.BlockSpec((None, all_rows, HEAD_SIZE), lambda g, p, o: (g, 0, 0))
    in_specs = [pl.BlockSpec((rows, width), lambda g, p, o: (p[0], g))]
    in_specs += [pl.BlockSpec((2, span, HEAD_SIZE), lambda g, p, o: (0, 0, g))] * len(arrays)
    scratch = [
        pltpu.VMEM((n_block, span, 2 * HEAD_SIZE), BF16),
        pltpu.VMEM((n_block, span, 2 * HEAD_SIZE), BF16),
        pltpu.VMEM((all_rows, 2 * HEAD_SIZE), BF16),
        pltpu.VMEM((all_rows, 2 * HEAD_SIZE), F32),
    ]
    if not first:
        in_specs += [state_spec, state_spec]
        arrays += list(state)
    if last:
        in_specs.append(pl.BlockSpec(memory_space=pl.ANY))
        arrays.append(weight)
        out_shape = [
            jax.ShapeDtypeStruct((rows, kv_heads * width), BF16),
            jax.ShapeDtypeStruct((rows, columns), BF16),
        ]
        out_specs = [
            pl.BlockSpec((rows, width), lambda g, p, o: (0, g)),
            pl.BlockSpec((rows, columns), lambda g, p, o: (0, 0)),
        ]
        scratch += [
            pltpu.VMEM((all_rows, HEAD_SIZE), F32),
            pltpu.VMEM((rows, kv_heads * width), BF16),
            pltpu.VMEM((weight.shape[0], columns), BF16),
            pltpu.SemaphoreType.DMA,
        ]
    else:
        out_shape = [pltpu.HBM((kv_heads, all_rows, HEAD_SIZE), F32)] * 2
        out_specs = [state_spec, state_spec]
    return pl.pallas_call(
        functools.partial(attention_kernel, slots, rows, group, min(rows, 256), first, last),
        out_shape=out_shape,
        grid_spec=pltpu.PrefetchScalarGridSpec(
            num_scalar_prefetch=2,
            grid=(kv_heads,),
            in_specs=in_specs,
            out_specs=out_specs,
            scratch_shapes=scratch,
        ),
        compiler_params=pltpu.CompilerParams(vmem_limit_bytes=48 * 2**20),
    )(place, older_count, queries, *arrays)


def project_kernel(n_part, a_ref, w_ref, *rest):
    total = jnp.dot(a_ref[...], w_ref[...], preferred_element_type=F32)
    if n_part == 0:
        rest[0][...] = total.astype(BF16)
        return
    gate_ref, residual_ref = rest[:2]
    for part in rest[2 : 2 + n_part]:
        total = total + part[...].astype(F32)
    rest[-1][...] = (residual_ref[...].astype(F32) + gate_ref[...] * total).astype(BF16)


def combine_kernel(n_part, gate_ref, residual_ref, *rest):
    total = rest[0][...].astype(F32)
    for part in rest[1:n_part]:
        total = total + part[...].astype(F32)
    rest[-1][...] = (residual_ref[...].astype(F32) + gate_ref[...] * total).astype(BF16)


def project(attended, weight, begin, columns, tile):
    rows, depth = attended.shape
    return pl.pallas_call(
        functools.partial(project_kernel, 0),
        out_shape=jax.ShapeDtypeStruct((rows, columns), BF16),
        grid=(columns // tile,),
        in_specs=[
            pl.BlockSpec((rows, depth), lambda i: (0, 0)),
            pl.BlockSpec((depth, tile), lambda i: (0, begin // tile + i)),
        ],
        out_specs=pl.BlockSpec((rows, tile), lambda i: (0, i)),
        compiler_params=pltpu.CompilerParams(vmem_limit_bytes=40 * 2**20),
    )(attended, weight)


def finish(operands, parts, gate_row, residual, begin, columns, tile, out):
    rows, width = residual.shape
    here = pl.BlockSpec((rows, tile), lambda i: (0, begin // tile + i))
    in_specs = []
    if operands:
        depth = operands[1].shape[0]
        in_specs += [pl.BlockSpec((rows, depth), lambda i: (0, 0))]
        in_specs += [pl.BlockSpec((depth, tile), lambda i: (0, begin // tile + i))]
    in_specs += [pl.BlockSpec((1, tile), lambda i: (0, begin // tile + i)), here]
    in_specs += [pl.BlockSpec((rows, tile), lambda i: (0, i))] * len(parts)
    arguments = [*operands, gate_row, residual, *parts]
    aliases = {}
    if out is not None:
        aliases = {len(arguments): 0}
        in_specs.append(pl.BlockSpec(memory_space=pl.ANY))
        arguments.append(out)
    kernel = project_kernel if operands else combine_kernel
    return pl.pallas_call(
        functools.partial(kernel, len(parts)),
        out_shape=jax.ShapeDtypeStruct((rows, width), BF16),
        grid=(columns // tile,),
        in_specs=in_specs,
        out_specs=here,
        input_output_aliases=aliases,
        compiler_params=pltpu.CompilerParams(vmem_limit_bytes=40 * 2**20),
    )(*arguments)


def move(block, n_span, sends, target):
    route = [(i, target(i)) for i in range(n_span) if sends(i) and 0 <= target(i) < n_span]
    return lax.ppermute(block, "span", route)


def on_device(
    queries,
    stacked_key_vectors,
    stacked_value_vectors,
    out_weight,
    residual,
    gate_table,
    noise_step,
    older_count,
):
    span_len = queries.shape[0]
    kv_heads = stacked_key_vectors.shape[1] // HEAD_SIZE
    group = queries.shape[1] // HEAD_SIZE // kv_heads
    model_width = out_weight.shape[1]
    n_span = lax.axis_size("span")
    n_head = lax.axis_size("head")
    my_span = lax.axis_index("span")
    my_head = lax.axis_index("head")
    rows = span_len // n_head

    own = jnp.stack([stacked_key_vectors, stacked_value_vectors])
    hop = functools.partial(move, n_span=n_span)
    places = [jnp.stack([(my_head + k) % n_head, my_span]).astype(jnp.int32) for k in range(n_head)]

    tile = model_width // 6
    chunks = [(0, 2), (2, 2), (4, 1), (5, 1)]
    first_columns = chunks[0][1] * tile

    def attend(k, blocks, state=None, last=False):
        weight = out_weight if last else None
        return attention(queries, places[k], older_count, rows, group, blocks, state, weight, first_columns)

    others = range(1, n_head)
    up = hop(own, sends=lambda i: True, target=lambda i: i + 4)
    across = hop(own, sends=lambda i: True, target=lambda i: i ^ 2)
    beside = hop(own, sends=lambda i: i & 1 == 0, target=lambda i: i ^ 1)
    states = [attend(k, {0: own}) for k in range(n_head)]
    up, across, beside, states = lax.optimization_barrier((up, across, beside, states))
    across_up = hop(across, sends=lambda i: i & 2 == 0, target=lambda i: i + 4)
    up_across = hop(up, sends=lambda i: i & 2 == 0, target=lambda i: i ^ 2)
    up_diagonal = hop(up, sends=lambda i: i & 2 > 0, target=lambda i: i + 2)
    up_seventh = hop(up, sends=lambda i: i & 1 > 0, target=lambda i: i + 3)
    across_beside = hop(across, sends=lambda i: i & 2 > 0, target=lambda i: i ^ 1)
    up_beside = hop(up, sends=lambda i: True, target=lambda i: i ^ 1)
    early = {1: beside, 2: across, 3: across_beside, 4: up, 5: up_beside}
    for k in others:
        states[k] = attend(k, early, states[k])
    across_up, up_across, up_diagonal, up_seventh, states = lax.optimization_barrier(
        (across_up, up_across, up_diagonal, up_seventh, states)
    )
    across_up_beside = hop(across_up, sends=lambda i: i & 2 == 0, target=lambda i: i ^ 1)
    up_across_beside = hop(up_across, sends=lambda i: i & 2 > 0, target=lambda i: i ^ 1)
    up_diagonal_beside = hop(up_diagonal, sends=lambda i: i & 2 == 0, target=lambda i: i ^ 1)
    late = {
        6: across_up,
        7: across_up_beside,
        8: up_across,
        9: up_across_beside,
        10: up_seventh,
        11: up_diagonal,
        12: up_diagonal_beside,
    }

    received = [[] for _ in chunks]
    for k in others:
        attended, partial = attend(k, late, states[k], last=True)
        route = [(i, (i + k) % n_head) for i in range(n_head)]
        received[0].append(lax.ppermute(partial, "head", route))
        for c, (begin, count) in list(enumerate(chunks))[1:]:
            partial = project(attended, out_weight, begin * tile, count * tile, tile)
            received[c].append(lax.ppermute(partial, "head", route))
            attended, partial = lax.optimization_barrier((attended, partial))

    states, attended = lax.optimization_barrier((states, attended))
    attended, kept = attend(0, {**early, **late}, states[0], last=True)
    gate_row = lax.dynamic_slice_in_dim(gate_table, noise_step[my_span], 1, 0)
    out = None
    for c, (begin, count) in enumerate(chunks):
        operands, parts = [], [kept, *received[c]]
        if c == len(chunks) - 1:
            parts = [project(attended, out_weight, begin * tile, count * tile, tile), *received[c]]
        elif c > 0:
            operands, parts = [attended, out_weight], received[c]
        out = finish(operands, parts, gate_row, residual, begin * tile, count * tile, tile, out)
    return out


def solution(mesh):
    in_specs = (
        P("span", "head"),
        P("span", "head"),
        P("span", "head"),
        P("head", None),
        P(("span", "head"), None),
        P(),
        P(),
        P(),
    )
    out_specs = P(("span", "head"), None)
    return jax.shard_map(
        on_device, mesh=mesh, in_specs=in_specs, out_specs=out_specs, check_vma=False
    )
```

time: 537 us -> 204 us (0.38)
  the two profiles are of different devices: /device:TPU:17 before, /device:TPU:16 now
where the time goes in v1:
time: 204 us; the launch traced here: 203 us
  Pallas kernels  143 us (70%)
  starting transfers between devices  28.3 us (14%)
  waiting for transfers between devices  19 us (9%)
  local copies, waits for them, and re-layouts  9.29 us (5%)
  between operations  2.44 us (1%)
    pallas_call x5, Pallas kernels, attention(): pl.pallas_call(functools.partial(attention_kernel, slots, rows, group, mi...  105 us
    ppermute x12, starting transfers between devices, move(): return lax.ppermute(block, 'span', route)  24 us
    pallas_call x4, Pallas kernels, project(): pl.pallas_call(functools.partial(project_kernel, 0), out_shape=jax.ShapeD...  21.2 us
    ppermute x12, waiting for transfers between devices, move(): return lax.ppermute(block, 'span', route)  18.9 us
    pallas_call x4, Pallas kernels, finish(): pl.pallas_call(functools.partial(kernel, len(parts)), out_shape=jax.Shape...  16.5 us
    unnamed x50, local copies, waits for them, and re-layouts  8.61 us
  transfers between devices with their start and end apart: 16, of which 5 were waited for; matrix products, arithmetic and copies ran while one was open for 0% of the time, Pallas kernels for 54%

profile of v1, /device:TPU:16, one launch (start us, length us, event | category | flops | bytes accessed | tf_op | source)
XLA Modules:
  0.0 203.3 jit_solution(8619559425522263570)
XLA Ops:
  0.0 1.4 pad_maximum_fusion.rest_0_
  1.4 1.8 collective-permute-start.2
  3.2 1.6 collective-permute-start.1
  4.8 3.5 %collective-permute-start = (bf16[2,512,512]{2,1,0:T(8,128)(2,1)S(1)}, bf16[2,512,512]{2,1,0:T(8,128)(2,1)}, u32[]{:S(2)}, u32[]{:S(2)}) collective-permute-start(bf16[2,512,512]{2,1,0:T(8,128)(2,1)S(1)} %pad_maximum_fusion.rest_0_), channel_id=1, source_target_pairs={{0,8},{2,10},{4,12},{6,14},{8,16},{10,18},{12,20},{14,22},{16,24},... | collective-permute-start | bytes 3145736 | tf_op jit(solution)/shard_map/ppermute | solution.py:287
  8.4 1.9 copy-done.2
  10.9 7.5 %shard_map.83 = (f32[4,1536,128]{2,1,0:T(8,128)}, f32[4,1536,128]{2,1,0:T(8,128)}) custom-call(s32[2]{0:T(128)S(1)} %get-tuple-element.64.place, s32[16]{0:T(128)S(1)} %copy-done.19, bf16[512,3072]{1,0:T(8,128)(2,1)S(1)} %copy-done.2, bf16[2,512,512]{2,1,0:T(8,128)(2,1)S(1)} %pad_maximum_fusion.rest_0_), custom_call_target="tpu_custom_call" | custom-call | tf_op jit(solution)/shard_map/pallas_call | solution.py:210
  18.5 7.5 %shard_map.82 = (f32[4,1536,128]{2,1,0:T(8,128)}, f32[4,1536,128]{2,1,0:T(8,128)}) custom-call(s32[2]{0:T(128)S(1)} %get-tuple-element.63.place, s32[16]{0:T(128)S(1)} %copy-done.20, bf16[512,3072]{1,0:T(8,128)(2,1)S(1)} %copy-done.3, bf16[2,512,512]{2,1,0:T(8,128)(2,1)S(1)} %pad_maximum_fusion.rest_0_), custom_call_target="tpu_custom_call" | custom-call | tf_op jit(solution)/shard_map/pallas_call | solution.py:210
  27.8 3.1 %collective-permute-done.rest_3_ = bf16[2,512,512]{2,1,0:T(8,128)(2,1)} collective-permute-done((bf16[2,512,512]{2,1,0:T(8,128)(2,1)S(1)}, bf16[2,512,512]{2,1,0:T(8,128)(2,1)}, u32[]{:S(2)}, u32[]{:S(2)}) %collective-permute-start) | collective-permute-done | bytes 1048608 | tf_op jit(solution)/shard_map/ppermute | solution.py:287
  31.7 3.5 %collective-permute-start.5 = (bf16[2,512,512]{2,1,0:T(8,128)(2,1)}, bf16[2,512,512]{2,1,0:T(8,128)(2,1)S(1)}, u32[]{:S(2)}, u32[]{:S(2)}) collective-permute-start(bf16[2,512,512]{2,1,0:T(8,128)(2,1)} %collective-permute-done.1.rest_1_), channel_id=1, source_target_pairs={{0,8},{2,10},{8,16},{10,18},{16,24},{18,26},{1,9},{3,11},{9,17},{1... | collective-permute-start | bytes 3145736 | tf_op jit(solution)/shard_map/ppermute | solution.py:287
  35.2 1.3 collective-permute-start.8
  36.5 1.3 collective-permute-start.7
  37.8 3.5 %collective-permute-start.6 = (bf16[2,512,512]{2,1,0:T(8,128)(2,1)}, bf16[2,512,512]{2,1,0:T(8,128)(2,1)S(1)}, u32[]{:S(2)}, u32[]{:S(2)}) collective-permute-start(bf16[2,512,512]{2,1,0:T(8,128)(2,1)} %collective-permute-done.rest_3_), channel_id=1, source_target_pairs={{0,4},{2,6},{8,12},{10,14},{16,20},{18,22},{24,28},{26,30},{1,5},{... | collective-permute-start | bytes 3145736 | tf_op jit(solution)/shard_map/ppermute | solution.py:287
  41.3 1.2 copy-done.14
  42.5 15.4 %shard_map.84 = (f32[4,1536,128]{2,1,0:T(8,128)}, f32[4,1536,128]{2,1,0:T(8,128)}) custom-call(s32[2]{0:T(128)S(1)} %get-tuple-element.64.place, s32[16]{0:T(128)S(1)} %copy-done.20, bf16[512,3072]{1,0:T(8,128)(2,1)} %q_ref.9, bf16[2,512,512]{2,1,0:T(8,128)(2,1)S(1)} %copy-done.14, bf16[2,512,512]{2,1,0:T(8,128)(2,1)} %collective-permute-done.1.rest_1_, ...), custom_call_target="tpu_custom_call" | custom-call | tf_op jit(solution)/shard_map/pallas_call | solution.py:210
  58.0 1.8 collective-permute-done.5.rest_5_.rest_0_
  59.7 10.8 %collective-permute-done.8.rest_9_.rest_4_ = bf16[2,512,512]{2,1,0:T(8,128)(2,1)S(1)} collective-permute-done((bf16[2,512,512]{2,1,0:T(8,128)(2,1)}, bf16[2,512,512]{2,1,0:T(8,128)(2,1)S(1)}, u32[]{:S(2)}, u32[]{:S(2)}) %collective-permute-start.8) | collective-permute-done | bytes 1048608 | tf_op jit(solution)/shard_map/ppermute | solution.py:287
  70.6 4.0 %collective-permute-start.9 = (bf16[2,512,512]{2,1,0:T(8,128)(2,1)S(1)}, bf16[2,512,512]{2,1,0:T(8,128)(2,1)S(1)}, u32[]{:S(2)}, u32[]{:S(2)}) collective-permute-start(bf16[2,512,512]{2,1,0:T(8,128)(2,1)S(1)} %collective-permute-done.5.rest_5_.rest_0_), channel_id=1, source_target_pairs={{0,2},{2,0},{8,10},{10,8},{16,18},{18,16},{24,26},{26,24},{1,3},{3... | collective-permute-start | bytes 3145736 | tf_op jit(solution)/shard_map/ppermute | solution.py:287
  75.3 2.1 %collective-permute-start.11 = (bf16[2,512,512]{2,1,0:T(8,128)(2,1)S(1)}, bf16[2,512,512]{2,1,0:T(8,128)(2,1)S(1)}, u32[]{:S(2)}, u32[]{:S(2)}) collective-permute-start(bf16[2,512,512]{2,1,0:T(8,128)(2,1)S(1)} %collective-permute-done.7.rest_10_.rest_5_), channel_id=1, source_target_pairs={{0,2},{2,0},{8,10},{10,8},{16,18},{18,16},{24,26},{26,24},{1,3},{3... | collective-permute-start | bytes 3145736 | tf_op jit(solution)/shard_map/ppermute | solution.py:287
  77.5 2.4 %collective-permute-done.11.rest_11_.rest_6_ = bf16[2,512,512]{2,1,0:T(8,128)(2,1)S(1)} collective-permute-done((bf16[2,512,512]{2,1,0:T(8,128)(2,1)S(1)}, bf16[2,512,512]{2,1,0:T(8,128)(2,1)S(1)}, u32[]{:S(2)}, u32[]{:S(2)}) %collective-permute-start.11) | collective-permute-done | bytes 1048608 | tf_op jit(solution)/shard_map/ppermute | solution.py:287
  80.9 33.0 %shard_map.87 = (bf16[256,3072]{1,0:T(8,128)(2,1)}, bf16[256,2048]{1,0:T(8,128)(2,1)}) custom-call(s32[2]{0:T(128)S(1)} %get-tuple-element.64.place, s32[16]{0:T(128)S(1)} %copy-done.20, bf16[512,3072]{1,0:T(8,128)(2,1)} %q_ref.9, bf16[2,512,512]{2,1,0:T(8,128)(2,1)S(1)} %collective-permute-done.5.rest_5_.rest_0_, ...), custom_call_target="tpu_custom_call" | custom-call | tf_op jit(solution)/shard_map/pallas_call | solution.py:210
  113.9 1.6 collective-permute-start.15
  115.5 1.4 copy-done.5
  116.9 7.4 %shard_map.88 = bf16[256,2048]{1,0:T(8,128)(2,1)} custom-call(bf16[256,3072]{1,0:T(8,128)(2,1)S(1)} %copy-done.5, bf16[3072,6144]{1,0:T(8,128)(2,1)} %w_ref.11), custom_call_target="tpu_custom_call" | custom-call | tf_op jit(solution)/shard_map/pallas_call | solution.py:244
  127.5 4.6 %shard_map.89 = bf16[256,1024]{1,0:T(8,128)(2,1)S(1)} custom-call(bf16[256,3072]{1,0:T(8,128)(2,1)S(1)} %copy-done.6, bf16[3072,6144]{1,0:T(8,128)(2,1)} %w_ref.11), custom_call_target="tpu_custom_call" | custom-call | tf_op jit(solution)/shard_map/pallas_call | solution.py:244
  132.1 1.5 collective-permute-start.13
  133.7 4.6 %shard_map.90 = bf16[256,1024]{1,0:T(8,128)(2,1)S(1)} custom-call(bf16[256,3072]{1,0:T(8,128)(2,1)S(1)} %copy-done.6, bf16[3072,6144]{1,0:T(8,128)(2,1)} %w_ref.11), custom_call_target="tpu_custom_call" | custom-call | tf_op jit(solution)/shard_map/pallas_call | solution.py:244
  138.9 41.8 %shard_map.85 = (bf16[256,3072]{1,0:T(8,128)(2,1)}, bf16[256,2048]{1,0:T(8,128)(2,1)S(1)}) custom-call(s32[2]{0:T(128)S(1)} %get-tuple-element.63.place, s32[16]{0:T(128)S(1)} %copy-done.20, bf16[512,3072]{1,0:T(8,128)(2,1)} %q_ref.9, bf16[2,512,512]{2,1,0:T(8,128)(2,1)S(1)} %copy-done.15, bf16[2,512,512]{2,1,0:T(8,128)(2,1)} %collective-permute-done.1.rest_1_, ...), custom_call_target="tpu_custom_call" | custom-call | tf_op jit(solution)/shard_map/pallas_call | solution.py:210
  180.7 1.4 copy-done.7
  182.1 4.7 %shard_map.86.rest_0_ = bf16[256,1024]{1,0:T(8,128)(2,1)S(1)} custom-call(bf16[256,3072]{1,0:T(8,128)(2,1)S(1)} %copy-done.7, bf16[3072,6144]{1,0:T(8,128)(2,1)} %w_ref.11), custom_call_target="tpu_custom_call" | custom-call | tf_op jit(solution)/shard_map/pallas_call | solution.py:244
  186.8 2.5 %shard_map.91.rest_3_ = bf16[256,6144]{1,0:T(8,128)(2,1)} custom-call(f32[1,6144]{1,0:T(1,128)S(1)} %constant_dynamic-slice_fusion.gate_ref.rest_0_, bf16[256,6144]{1,0:T(8,128)(2,1)S(1)} %copy-done.4, bf16[256,2048]{1,0:T(8,128)(2,1)S(1)} %get-tuple-element.61.rest_0_, bf16[256,2048]{1,0:T(8,128)(2,1)} %collective-permute-done.15.rest_1_), custom_call_target="tpu_custom_call" | custom-call | tf_op jit(solution)/shard_map/pallas_call | solution.py:274
  189.3 7.4 %shard_map.92.rest_3_ = bf16[256,6144]{1,0:T(8,128)(2,1)} custom-call(bf16[256,3072]{1,0:T(8,128)(2,1)S(1)} %copy-done.8, bf16[3072,6144]{1,0:T(8,128)(2,1)} %w_ref.11, f32[1,6144]{1,0:T(1,128)S(1)} %constant_dynamic-slice_fusion.gate_ref.rest_0_, bf16[256,6144]{1,0:T(8,128)(2,1)S(1)} %copy-done.4, ...), custom_call_target="tpu_custom_call", output_to_operand_aliasing={{}: (5, {})} | custom-call | tf_op jit(solution)/shard_map/pallas_call | solution.py:274
  196.8 5.5 %shard_map.93.rest_2_ = bf16[256,6144]{1,0:T(8,128)(2,1)} custom-call(bf16[256,3072]{1,0:T(8,128)(2,1)S(1)} %copy-done.8, bf16[3072,6144]{1,0:T(8,128)(2,1)} %w_ref.11, f32[1,6144]{1,0:T(1,128)S(1)} %constant_dynamic-slice_fusion.gate_ref.rest_0_, bf16[256,6144]{1,0:T(8,128)(2,1)S(1)} %copy-done.4, ...), custom_call_target="tpu_custom_call", output_to_operand_aliasing={{}: (5, {})} | custom-call | tf_op jit(solution)/shard_map/pallas_call | solution.py:274
  (67 shorter events, 8.0 us)
Async XLA Ops:
  0.0 138.8 %copy-start = (f32[32,6144]{1,0:T(8,128)S(1)}, f32[32,6144]{1,0:T(8,128)}, u32[]{:S(2)}) copy-start(f32[32,6144]{1,0:T(8,128)} %param.13) | copy-start | bytes 2359300
  0.0 18.5 %copy-start.20 = (s32[16]{0:T(128)S(1)}, s32[16]{0:T(128)}, u32[]{:S(2)}) copy-start(s32[16]{0:T(128)} %older_count.9) | copy-start | bytes 196
  1.4 24.6 %collective-permute-start.2 = (bf16[2,512,512]{2,1,0:T(8,128)(2,1)S(1)}, bf16[2,512,512]{2,1,0:T(8,128)(2,1)S(1)}, u32[]{:S(2)}, u32[]{:S(2)}) collective-permute-start(bf16[2,512,512]{2,1,0:T(8,128)(2,1)S(1)} %pad_maximum_fusion.rest_0_), channel_id=1, source_target_pairs={{0,2},{4,6},{8,10},{12,14},{16,18},{20,22},{24,26},{28,30},{1,3},{... | collective-permute-start | bytes 3145736 | tf_op jit(solution)/shard_map/ppermute | solution.py:287
  3.2 24.6 %collective-permute-start.1 = (bf16[2,512,512]{2,1,0:T(8,128)(2,1)S(1)}, bf16[2,512,512]{2,1,0:T(8,128)(2,1)}, u32[]{:S(2)}, u32[]{:S(2)}) collective-permute-start(bf16[2,512,512]{2,1,0:T(8,128)(2,1)S(1)} %pad_maximum_fusion.rest_0_), channel_id=1, source_target_pairs={{0,4},{2,6},{4,0},{6,2},{8,12},{10,14},{12,8},{14,10},{16,20},{18,... | collective-permute-start | bytes 3145736 | tf_op jit(solution)/shard_map/ppermute | solution.py:287
  4.8 26.1 %collective-permute-start = (bf16[2,512,512]{2,1,0:T(8,128)(2,1)S(1)}, bf16[2,512,512]{2,1,0:T(8,128)(2,1)}, u32[]{:S(2)}, u32[]{:S(2)}) collective-permute-start(bf16[2,512,512]{2,1,0:T(8,128)(2,1)S(1)} %pad_maximum_fusion.rest_0_), channel_id=1, source_target_pairs={{0,8},{2,10},{4,12},{6,14},{8,16},{10,18},{12,20},{14,22},{16,24},... | collective-permute-start | bytes 3145736 | tf_op jit(solution)/shard_map/ppermute | solution.py:287
  10.9 7.6 %copy-start.3 = (bf16[512,3072]{1,0:T(8,128)(2,1)S(1)}, bf16[512,3072]{1,0:T(8,128)(2,1)}, u32[]{:S(2)}) copy-start(bf16[512,3072]{1,0:T(8,128)(2,1)} %q_ref.9) | copy-start | bytes 9437188
  30.9 6.9 %collective-permute-start.3 = (bf16[2,512,512]{2,1,0:T(8,128)(2,1)}, bf16[2,512,512]{2,1,0:T(8,128)(2,1)S(1)}, u32[]{:S(2)}, u32[]{:S(2)}) collective-permute-start(bf16[2,512,512]{2,1,0:T(8,128)(2,1)} %collective-permute-done.1.rest_1_), channel_id=1, source_target_pairs={{4,6},{6,4},{12,14},{14,12},{20,22},{22,20},{28,30},{30,28},{5,7},... | collective-permute-start | bytes 3145736 | tf_op jit(solution)/shard_map/ppermute | solution.py:287
  31.6 9.7 %collective-permute-start.4 = (bf16[2,512,512]{2,1,0:T(8,128)(2,1)}, bf16[2,512,512]{2,1,0:T(8,128)(2,1)S(1)}, u32[]{:S(2)}, u32[]{:S(2)}) collective-permute-start(bf16[2,512,512]{2,1,0:T(8,128)(2,1)} %collective-permute-done.rest_3_), channel_id=1, source_target_pairs={{0,2},{2,0},{4,6},{6,4},{8,10},{10,8},{12,14},{14,12},{16,18},{18,... | collective-permute-start | bytes 3145736 | tf_op jit(solution)/shard_map/ppermute | solution.py:287
  31.7 28.1 %collective-permute-start.5 = (bf16[2,512,512]{2,1,0:T(8,128)(2,1)}, bf16[2,512,512]{2,1,0:T(8,128)(2,1)S(1)}, u32[]{:S(2)}, u32[]{:S(2)}) collective-permute-start(bf16[2,512,512]{2,1,0:T(8,128)(2,1)} %collective-permute-done.1.rest_1_), channel_id=1, source_target_pairs={{0,8},{2,10},{8,16},{10,18},{16,24},{18,26},{1,9},{3,11},{9,17},{1... | collective-permute-start | bytes 3145736 | tf_op jit(solution)/shard_map/ppermute | solution.py:287
  35.2 35.4 %collective-permute-start.8 = (bf16[2,512,512]{2,1,0:T(8,128)(2,1)}, bf16[2,512,512]{2,1,0:T(8,128)(2,1)S(1)}, u32[]{:S(2)}, u32[]{:S(2)}) collective-permute-start(bf16[2,512,512]{2,1,0:T(8,128)(2,1)} %collective-permute-done.rest_3_), channel_id=1, source_target_pairs={{2,8},{6,12},{10,16},{14,20},{18,24},{22,28},{3,9},{7,13},{11,17},... | collective-permute-start | bytes 3145736 | tf_op jit(solution)/shard_map/ppermute | solution.py:287
  36.5 34.1 %collective-permute-start.7 = (bf16[2,512,512]{2,1,0:T(8,128)(2,1)}, bf16[2,512,512]{2,1,0:T(8,128)(2,1)S(1)}, u32[]{:S(2)}, u32[]{:S(2)}) collective-permute-start(bf16[2,512,512]{2,1,0:T(8,128)(2,1)} %collective-permute-done.rest_3_), channel_id=1, source_target_pairs={{4,8},{6,10},{12,16},{14,18},{20,24},{22,26},{5,9},{7,11},{13,17},... | collective-permute-start | bytes 3145736 | tf_op jit(solution)/shard_map/ppermute | solution.py:287
  37.8 20.2 %copy-start.16 = (bf16[2,512,512]{2,1,0:T(8,128)(2,1)}, bf16[2,512,512]{2,1,0:T(8,128)(2,1)S(1)}, u32[]{:S(2)}) copy-start(bf16[2,512,512]{2,1,0:T(8,128)(2,1)S(1)} %collective-permute-done.3.rest_2_) | copy-start | bytes 3145732
  37.8 32.8 %collective-permute-start.6 = (bf16[2,512,512]{2,1,0:T(8,128)(2,1)}, bf16[2,512,512]{2,1,0:T(8,128)(2,1)S(1)}, u32[]{:S(2)}, u32[]{:S(2)}) collective-permute-start(bf16[2,512,512]{2,1,0:T(8,128)(2,1)} %collective-permute-done.rest_3_), channel_id=1, source_target_pairs={{0,4},{2,6},{8,12},{10,14},{16,20},{18,22},{24,28},{26,30},{1,5},{... | collective-permute-start | bytes 3145736 | tf_op jit(solution)/shard_map/ppermute | solution.py:287
  42.5 15.4 %copy-start.18 = (bf16[2,512,512]{2,1,0:T(8,128)(2,1)}, bf16[2,512,512]{2,1,0:T(8,128)(2,1)S(1)}, u32[]{:S(2)}) copy-start(bf16[2,512,512]{2,1,0:T(8,128)(2,1)S(1)} %collective-permute-done.4.rest_4_) | copy-start | bytes 3145732
  59.7 54.1 %copy-start.9 = (bf16[2,512,512]{2,1,0:T(8,128)(2,1)}, bf16[2,512,512]{2,1,0:T(8,128)(2,1)S(1)}, u32[]{:S(2)}) copy-start(bf16[2,512,512]{2,1,0:T(8,128)(2,1)S(1)} %collective-permute-done.5.rest_5_.rest_0_) | copy-start | bytes 3145732
  70.6 9.3 %copy-start.21 = (bf16[2,512,512]{2,1,0:T(8,128)(2,1)}, bf16[2,512,512]{2,1,0:T(8,128)(2,1)S(1)}, u32[]{:S(2)}) copy-start(bf16[2,512,512]{2,1,0:T(8,128)(2,1)S(1)} %collective-permute-done.8.rest_9_.rest_4_) | copy-start | bytes 3145732
  70.6 9.3 %copy-start.22 = (bf16[2,512,512]{2,1,0:T(8,128)(2,1)}, bf16[2,512,512]{2,1,0:T(8,128)(2,1)S(1)}, u32[]{:S(2)}) copy-start(bf16[2,512,512]{2,1,0:T(8,128)(2,1)S(1)} %collective-permute-done.7.rest_10_.rest_5_) | copy-start | bytes 3145732
  70.6 43.3 %copy-start.10 = (bf16[2,512,512]{2,1,0:T(8,128)(2,1)}, bf16[2,512,512]{2,1,0:T(8,128)(2,1)S(1)}, u32[]{:S(2)}) copy-start(bf16[2,512,512]{2,1,0:T(8,128)(2,1)S(1)} %collective-permute-done.6.rest_7_.rest_2_) | copy-start | bytes 3145732
  70.6 6.8 %collective-permute-start.9 = (bf16[2,512,512]{2,1,0:T(8,128)(2,1)S(1)}, bf16[2,512,512]{2,1,0:T(8,128)(2,1)S(1)}, u32[]{:S(2)}, u32[]{:S(2)}) collective-permute-start(bf16[2,512,512]{2,1,0:T(8,128)(2,1)S(1)} %collective-permute-done.5.rest_5_.rest_0_), channel_id=1, source_target_pairs={{0,2},{2,0},{8,10},{10,8},{16,18},{18,16},{24,26},{26,24},{1,3},{3... | collective-permute-start | bytes 3145736 | tf_op jit(solution)/shard_map/ppermute | solution.py:287
  74.6 2.9 %collective-permute-start.10 = (bf16[2,512,512]{2,1,0:T(8,128)(2,1)S(1)}, bf16[2,512,512]{2,1,0:T(8,128)(2,1)S(1)}, u32[]{:S(2)}, u32[]{:S(2)}) collective-permute-start(bf16[2,512,512]{2,1,0:T(8,128)(2,1)S(1)} %collective-permute-done.6.rest_7_.rest_2_), channel_id=1, source_target_pairs={{4,6},{6,4},{12,14},{14,12},{20,22},{22,20},{28,30},{30,28},{5,7},... | collective-permute-start | bytes 3145736 | tf_op jit(solution)/shard_map/ppermute | solution.py:287
  75.3 4.6 %collective-permute-start.11 = (bf16[2,512,512]{2,1,0:T(8,128)(2,1)S(1)}, bf16[2,512,512]{2,1,0:T(8,128)(2,1)S(1)}, u32[]{:S(2)}, u32[]{:S(2)}) collective-permute-start(bf16[2,512,512]{2,1,0:T(8,128)(2,1)S(1)} %collective-permute-done.7.rest_10_.rest_5_), channel_id=1, source_target_pairs={{0,2},{2,0},{8,10},{10,8},{16,18},{18,16},{24,26},{26,24},{1,3},{3... | collective-permute-start | bytes 3145736 | tf_op jit(solution)/shard_map/ppermute | solution.py:287
  77.4 36.5 %copy-start.11 = (bf16[2,512,512]{2,1,0:T(8,128)(2,1)}, bf16[2,512,512]{2,1,0:T(8,128)(2,1)S(1)}, u32[]{:S(2)}) copy-start(bf16[2,512,512]{2,1,0:T(8,128)(2,1)S(1)} %collective-permute-done.9.rest_6_.rest_1_) | copy-start | bytes 3145732
  77.4 36.4 %copy-start.12 = (bf16[2,512,512]{2,1,0:T(8,128)(2,1)}, bf16[2,512,512]{2,1,0:T(8,128)(2,1)S(1)}, u32[]{:S(2)}) copy-start(bf16[2,512,512]{2,1,0:T(8,128)(2,1)S(1)} %collective-permute-done.10.rest_8_.rest_3_) | copy-start | bytes 3145732
  113.9 72.9 %collective-permute-start.15 = (bf16[256,2048]{1,0:T(8,128)(2,1)}, bf16[256,2048]{1,0:T(8,128)(2,1)}, u32[]{:S(2)}, u32[]{:S(2)}) collective-permute-start(bf16[256,2048]{1,0:T(8,128)(2,1)} %get-tuple-element.62), channel_id=1, source_target_pairs={{0,1},{1,0},{2,3},{3,2},{4,5},{5,4},{6,7},{7,6},{8,9},{9,8},{10,11... | collective-permute-start | bytes 3145736 | tf_op jit(solution)/shard_map/ppermute | solution.py:357
  116.9 7.9 %copy-start.24 = (s32[16]{0:T(128)S(1)}, s32[16]{0:T(128)}, u32[]{:S(2)}) copy-start(s32[16]{0:T(128)} %param.14) | copy-start | bytes 196
  116.9 10.6 %copy-start.6 = (bf16[256,3072]{1,0:T(8,128)(2,1)S(1)}, bf16[256,3072]{1,0:T(8,128)(2,1)}, u32[]{:S(2)}) copy-start(bf16[256,3072]{1,0:T(8,128)(2,1)} %get-tuple-element.60.a_ref) | copy-start | bytes 4718596
  124.2 65.1 %collective-permute-start.14 = (bf16[256,2048]{1,0:T(8,128)(2,1)}, bf16[256,2048]{1,0:T(8,128)(2,1)S(1)}, u32[]{:S(2)}, u32[]{:S(2)}) collective-permute-start(bf16[256,2048]{1,0:T(8,128)(2,1)} %shard_map.88), channel_id=1, source_target_pairs={{0,1},{1,0},{2,3},{3,2},{4,5},{5,4},{6,7},{7,6},{8,9},{9,8},{10,11... | collective-permute-start | bytes 3145736 | tf_op jit(solution)/shard_map/ppermute | solution.py:360
  132.1 6.8 %copy-start.15 = (bf16[2,512,512]{2,1,0:T(8,128)(2,1)S(1)}, bf16[2,512,512]{2,1,0:T(8,128)(2,1)}, u32[]{:S(2)}) copy-start(bf16[2,512,512]{2,1,0:T(8,128)(2,1)} %copy-done.13) | copy-start | bytes 3145732
  132.1 6.8 %copy-start.17 = (bf16[2,512,512]{2,1,0:T(8,128)(2,1)S(1)}, bf16[2,512,512]{2,1,0:T(8,128)(2,1)}, u32[]{:S(2)}) copy-start(bf16[2,512,512]{2,1,0:T(8,128)(2,1)} %copy-done.16) | copy-start | bytes 3145732
  132.1 64.6 %collective-permute-start.13 = (bf16[256,1024]{1,0:T(8,128)(2,1)S(1)}, bf16[256,1024]{1,0:T(8,128)(2,1)S(1)}, u32[]{:S(2)}, u32[]{:S(2)}) collective-permute-start(bf16[256,1024]{1,0:T(8,128)(2,1)S(1)} %shard_map.89), channel_id=1, source_target_pairs={{0,1},{1,0},{2,3},{3,2},{4,5},{5,4},{6,7},{7,6},{8,9},{9,8},{10,11... | collective-permute-start | bytes 1572872 | tf_op jit(solution)/shard_map/ppermute | solution.py:360
  138.2 64.1 %collective-permute-start.12 = (bf16[256,1024]{1,0:T(8,128)(2,1)S(1)}, bf16[256,1024]{1,0:T(8,128)(2,1)S(1)}, u32[]{:S(2)}, u32[]{:S(2)}) collective-permute-start(bf16[256,1024]{1,0:T(8,128)(2,1)S(1)} %shard_map.90), channel_id=1, source_target_pairs={{0,1},{1,0},{2,3},{3,2},{4,5},{5,4},{6,7},{7,6},{8,9},{9,8},{10,11... | collective-permute-start | bytes 1572872 | tf_op jit(solution)/shard_map/ppermute | solution.py:360
  196.8 6.6 %copy-start.1 = (f32[32,6144]{1,0:T(8,128)S(1)}, f32[32,6144]{1,0:T(8,128)}, u32[]{:S(2)}) copy-start(f32[32,6144]{1,0:T(8,128)} %param.13) | copy-start | bytes 2359300
  (9 other events, 15.8 us)

commit v2 on v1

v2 whole, which is shorter than its diff:
```python
import functools
import math

import jax
import jax.numpy as jnp
from jax import lax
from jax.experimental import pallas as pl
from jax.experimental.pallas import tpu as pltpu
from jax.sharding import PartitionSpec as P

HEAD_SIZE = 128
MAX_BLOCKS = 8
EXPONENT_SCALE = math.log2(math.e) / math.sqrt(HEAD_SIZE)
TOTAL_LIMIT = 2.0**100
F32 = jnp.float32
BF16 = jnp.bfloat16


def slot_source(slot, my_span):
    core, y = my_span & 1, (my_span >> 1) & 1
    plane = my_span - 4
    return [
        (my_span, y >= 0),
        (my_span ^ 1, core == 1),
        (my_span ^ 2, y == 1),
        (my_span ^ 3, y == 1),
        (plane, y >= 0),
        (plane ^ 1, y >= 0),
        (plane ^ 2, y == 0),
        (plane ^ 3, y == 0),
        (plane ^ 2, y == 1),
        (plane ^ 3, y == 1),
        (my_span - 7, core == 0),
        (my_span - 6, y == 0),
        ((my_span - 6) ^ 1, y == 0),
    ][slot]


def attention_kernel(slots, rows, group, first, last, place, older_count, q_ref, *rest):
    kv_refs, rest = rest[: len(slots)], rest[len(slots) :]
    if not first:
        (sum_in, mark_in), rest = rest[:2], rest[2:]
    if last:
        weight_ref, out_ref, product_ref, keys, values, block_sems, scaled, acc, mark, attended, near_weight, arrived = rest
    else:
        sum_out, mark, keys, values, block_sems, scaled, acc = rest
    head = pl.program_id(0)
    n_head = pl.num_programs(0)
    now = lax.rem(head, 2)
    span = kv_refs[0].shape[1]
    all_rows = group * rows
    my_span = place[1]
    older_mine = older_count[my_span]

    places = []
    count = jnp.int32(0)
    for slot in slots:
        if slot == 0:
            seen = my_span >= 0
        else:
            source, used = slot_source(slot, my_span)
            seen = used & (source < my_span) & (my_span - source <= older_mine)
        places.append((seen, count))
        count = count + jnp.where(seen, 1, 0).astype(jnp.int32)

    def each_block(which, buffer, condition, act):
        columns = pl.ds(pl.multiple_of(which * HEAD_SIZE, HEAD_SIZE), HEAD_SIZE)
        left, right = pl.ds(0, HEAD_SIZE), pl.ds(HEAD_SIZE, HEAD_SIZE)
        for j, (seen, at) in enumerate(places):
            key_source = kv_refs[j].at[0, :, columns]
            copies = [(key_source, keys.at[buffer, at, :, left]), (key_source, keys.at[buffer, at, :, right])]
            for begin in range(0, span, HEAD_SIZE):
                part = pl.ds(begin, HEAD_SIZE)
                copies.append((kv_refs[j].at[1, part, columns], values.at[buffer, at, left, part]))
            copies = [
                pltpu.make_async_copy(source, target, block_sems.at[buffer, j, n])
                for n, (source, target) in enumerate(copies)
            ]

            @pl.when(seen & condition)
            def _():
                for copy in copies:
                    act(copy)

    each_block(head, now, head == 0, lambda copy: copy.start())
    each_block(head + 1, 1 - now, head + 1 < n_head, lambda copy: copy.start())
    if last:
        load = pltpu.make_async_copy(weight_ref.at[:, pl.ds(0, near_weight.shape[1])], near_weight, arrived)
        pl.when(head == 0)(load.start)

    @pl.when(head == 0)
    def _():
        values[:, :, HEAD_SIZE:, :] = jnp.ones(values.shape[:2] + (values.shape[2] - HEAD_SIZE, span), BF16)

    def scale():
        for h in range(group):
            q = q_ref[:, h * HEAD_SIZE : (h + 1) * HEAD_SIZE].astype(F32) * EXPONENT_SCALE
            q = q.T
            high = q.astype(BF16)
            scaled[:HEAD_SIZE, h * rows : (h + 1) * rows] = high
            scaled[HEAD_SIZE:, h * rows : (h + 1) * rows] = (q - high.astype(F32)).astype(BF16)

    def scores(block, at=slice(None)):
        return jnp.dot(keys[now, block], scaled[:, at], preferred_element_type=F32)

    def weigh(block, p):
        return jnp.dot(values[now, block], p.astype(BF16), preferred_element_type=F32)

    def add_block(block):
        acc[...] += weigh(block, jnp.exp2(scores(block) - mark[1:2, :]))

    if first:
        scale()
        each_block(head, now, head >= 0, lambda copy: copy.wait())
        s = scores(0)
        top = jnp.max(s, axis=0, keepdims=True)
        mark[0:1, :] = jnp.zeros((1, all_rows), F32)
        mark[1:2, :] = top
        acc[...] = weigh(0, jnp.exp2(s - top))
    else:
        pl.when(count > 0)(scale)
        acc[:HEAD_SIZE, :] = sum_in[...]
        acc[HEAD_SIZE:, :] = jnp.zeros((acc.shape[0] - HEAD_SIZE, all_rows), F32)
        mark[...] = mark_in[...]
        each_block(head, now, head >= 0, lambda copy: copy.wait())

    begin = 1 if first else 0
    if len(slots) > begin:
        pairs = (count - begin) // 2

        def two_blocks(i, carry):
            add_block(begin + 2 * i)
            add_block(begin + 2 * i + 1)
            return carry

        lax.fori_loop(0, pairs, two_blocks, 0)
        pl.when(begin + 2 * pairs < count)(functools.partial(add_block, count - 1))

        @pl.when(jnp.logical_not(jnp.max(acc[HEAD_SIZE : HEAD_SIZE + 8, :]) < TOTAL_LIMIT))
        def _():
            sub = math.gcd(all_rows, 384)

            def again(i, carry):
                at = pl.ds(pl.multiple_of(i * sub, sub), sub)
                acc[:, at] = jnp.zeros((acc.shape[0], sub), F32)
                if first:
                    mark[1:2, at] = jnp.full((1, sub), -1e30, F32)
                else:
                    acc[:HEAD_SIZE, at] = sum_in[:, at]
                    mark[:, at] = mark_in[:, at]

                def block_step(block, inner):
                    s = scores(block, at)
                    old_top = mark[1:2, at]
                    new_top = jnp.maximum(old_top, jnp.max(s, axis=0, keepdims=True))
                    shrink = jnp.exp2(old_top - new_top)
                    mark[0:1, at] = mark[0:1, at] * shrink
                    mark[1:2, at] = new_top
                    acc[:, at] = acc[:, at] * shrink + weigh(block, jnp.exp2(s - new_top))
                    return inner

                return lax.fori_loop(0, count, block_step, carry)

            lax.fori_loop(0, all_rows // sub, again, 0)

    total = mark[0:1, :] + acc[HEAD_SIZE : HEAD_SIZE + 1, :]
    if not last:
        mark[0:1, :] = total
        sum_out[...] = acc[:HEAD_SIZE, :]
        return
    for h in range(group):
        at = slice(h * rows, (h + 1) * rows)
        result = (acc[:HEAD_SIZE, at] / total[:, at]).T.astype(BF16)
        out_ref[:, h * HEAD_SIZE : (h + 1) * HEAD_SIZE] = result
        here = (head * group + h) * HEAD_SIZE
        attended[:, pl.ds(pl.multiple_of(here, HEAD_SIZE), HEAD_SIZE)] = result

    @pl.when(head == n_head - 1)
    def _():
        load.wait()
        tile = 512
        for begin in range(0, product_ref.shape[1], tile):
            at = slice(begin, begin + tile)
            product = jnp.dot(attended[...], near_weight[:, at], preferred_element_type=F32)
            product_ref[:, at] = product.astype(BF16)


def attention(queries, place, older_count, rows, group, blocks, state=None, weight=None, columns=0):
    slots = sorted(blocks)
    arrays = [blocks[slot] for slot in slots]
    first = state is None
    last = weight is not None
    kv_heads = arrays[0].shape[2] // HEAD_SIZE
    span = arrays[0].shape[1]
    width = group * HEAD_SIZE
    all_rows = group * rows
    n_block = min(MAX_BLOCKS, len(arrays))
    state_specs = [
        pl.BlockSpec((None, HEAD_SIZE, all_rows), lambda g, p, o: (g, 0, 0)),
        pl.BlockSpec((None, 8, all_rows), lambda g, p, o: (g, 0, 0)),
    ]
    high = HEAD_SIZE + 16
    in_specs = [pl.BlockSpec((rows, width), lambda g, p, o: (p[0], g))]
    in_specs += [pl.BlockSpec(memory_space=pltpu.HBM)] * len(arrays)
    scratch = [
        pltpu.VMEM((2, n_block, span, 2 * HEAD_SIZE), BF16),
        pltpu.VMEM((2, n_block, high, span), BF16),
        pltpu.SemaphoreType.DMA((2, len(arrays), 2 + span // HEAD_SIZE)),
        pltpu.VMEM((2 * HEAD_SIZE, all_rows), BF16),
        pltpu.VMEM((high, all_rows), F32),
    ]
    if not first:
        in_specs += state_specs
        arrays += list(state)
    if last:
        in_specs.append(pl.BlockSpec(memory_space=pltpu.HBM))
        arrays.append(weight)
        out_shape = [
            jax.ShapeDtypeStruct((rows, kv_heads * width), BF16),
            jax.ShapeDtypeStruct((rows, columns), BF16),
        ]
        out_specs = [
            pl.BlockSpec((rows, width), lambda g, p, o: (0, g)),
            pl.BlockSpec((rows, columns), lambda g, p, o: (0, 0)),
        ]
        scratch += [
            pltpu.VMEM((8, all_rows), F32),
            pltpu.VMEM((rows, kv_heads * width), BF16),
            pltpu.VMEM((weight.shape[0], columns), BF16),
            pltpu.SemaphoreType.DMA,
        ]
    else:
        out_shape = [pltpu.HBM((kv_heads, n, all_rows), F32) for n in (HEAD_SIZE, 8)]
        out_specs = state_specs
    return pl.pallas_call(
        functools.partial(attention_kernel, slots, rows, group, first, last),
        out_shape=out_shape,
        grid_spec=pltpu.PrefetchScalarGridSpec(
            num_scalar_prefetch=2,
            grid=(kv_heads,),
            in_specs=in_specs,
            out_specs=out_specs,
            scratch_shapes=scratch,
        ),
        compiler_params=pltpu.CompilerParams(vmem_limit_bytes=56 * 2**20),
    )(place, older_count, queries, *arrays)


def project_kernel(steps, a_ref, w_ref, *out_refs):
    step = pl.program_id(0)
    product = jnp.dot(a_ref[...], w_ref[...], preferred_element_type=F32).astype(BF16)
    for n, out_ref in enumerate(out_refs):

        @pl.when((step >= n * steps) & (step < (n + 1) * steps))
        def _(out_ref=out_ref):
            out_ref[...] = product


def project(attended, weight, begin, columns, n_out, tile):
    rows, depth = attended.shape
    steps = columns // tile
    return pl.pallas_call(
        functools.partial(project_kernel, steps),
        out_shape=[jax.ShapeDtypeStruct((rows, columns), BF16)] * n_out,
        grid=(n_out * steps,),
        in_specs=[
            pl.BlockSpec((rows, depth), lambda i: (0, 0)),
            pl.BlockSpec((depth, tile), lambda i: (0, begin // tile + i)),
        ],
        out_specs=[
            pl.BlockSpec((rows, tile), lambda i, n=n: (0, jnp.clip(i - n * steps, 0, steps - 1))) for n in range(n_out)
        ],
        compiler_params=pltpu.CompilerParams(vmem_limit_bytes=40 * 2**20),
    )(attended, weight)


def combine_kernel(n_part, place, noise_step, gate_ref, residual_ref, *rest):
    gate = gate_ref[pl.ds(noise_step[place[1]], 1), :]
    total = rest[0][...].astype(F32)
    for part in rest[1:n_part]:
        total = total + part[...].astype(F32)
    rest[-1][...] = (residual_ref[...].astype(F32) + gate * total).astype(BF16)


def combine(place, noise_step, gate_table, residual, kept, kept_begin, parts, begin, columns, tile, out):
    rows, width = residual.shape
    here = pl.BlockSpec((rows, tile), lambda i, p, n: (0, begin // tile + i))
    in_specs = [pl.BlockSpec((gate_table.shape[0], tile), lambda i, p, n: (0, begin // tile + i)), here]
    in_specs += [pl.BlockSpec((rows, tile), lambda i, p, n: (0, kept_begin // tile + i))]
    in_specs += [pl.BlockSpec((rows, tile), lambda i, p, n: (0, i))] * len(parts)
    arguments = [place, noise_step, gate_table, residual, kept, *parts]
    aliases = {}
    if out is not None:
        aliases = {len(arguments): 0}
        in_specs.append(pl.BlockSpec(memory_space=pl.ANY))
        arguments.append(out)
    return pl.pallas_call(
        functools.partial(combine_kernel, 1 + len(parts)),
        out_shape=jax.ShapeDtypeStruct((rows, width), BF16),
        grid_spec=pltpu.PrefetchScalarGridSpec(
            num_scalar_prefetch=2, grid=(columns // tile,), in_specs=in_specs, out_specs=here
        ),
        input_output_aliases=aliases,
        compiler_params=pltpu.CompilerParams(vmem_limit_bytes=40 * 2**20),
    )(*arguments)


def move(block, n_span, sends, target):
    route = [(i, target(i)) for i in range(n_span) if sends(i) and 0 <= target(i) < n_span]
    return lax.ppermute(block, "span", route)


def on_device(
    queries,
    stacked_key_vectors,
    stacked_value_vectors,
    out_weight,
    residual,
    gate_table,
    noise_step,
    older_count,
):
    span_len = queries.shape[0]
    kv_heads = stacked_key_vectors.shape[1] // HEAD_SIZE
    group = queries.shape[1] // HEAD_SIZE // kv_heads
    model_width = out_weight.shape[1]
    n_span = lax.axis_size("span")
    n_head = lax.axis_size("head")
    my_span = lax.axis_index("span")
    my_head = lax.axis_index("head")
    rows = span_len // n_head

    tiles = stacked_value_vectors.reshape(span_len // HEAD_SIZE, HEAD_SIZE, kv_heads, HEAD_SIZE)
    own = jnp.stack([stacked_key_vectors, tiles.transpose(0, 3, 2, 1).reshape(stacked_value_vectors.shape)])
    hop = functools.partial(move, n_span=n_span)
    places = [jnp.stack([(my_head + k) % n_head, my_span]).astype(jnp.int32) for k in range(n_head)]

    tile = model_width // 6
    chunk = 2 * tile

    def attend(k, blocks, state=None, columns=0):
        weight = out_weight if columns else None
        return attention(queries, places[k], older_count, rows, group, blocks, state, weight, columns)

    others = range(1, n_head)
    up = hop(own, sends=lambda i: True, target=lambda i: i + 4)
    across = hop(own, sends=lambda i: True, target=lambda i: i ^ 2)
    beside = hop(own, sends=lambda i: i & 1 == 0, target=lambda i: i ^ 1)
    states = [attend(k, {0: own}) for k in range(n_head)]
    up, across, beside, states = lax.optimization_barrier((up, across, beside, states))
    across_up = hop(across, sends=lambda i: i & 2 == 0, target=lambda i: i + 4)
    up_across = hop(up, sends=lambda i: i & 2 == 0, target=lambda i: i ^ 2)
    up_diagonal = hop(up, sends=lambda i: i & 2 > 0, target=lambda i: i + 2)
    up_seventh = hop(up, sends=lambda i: i & 1 > 0, target=lambda i: i + 3)
    across_beside = hop(across, sends=lambda i: i & 2 > 0, target=lambda i: i ^ 1)
    up_beside = hop(up, sends=lambda i: True, target=lambda i: i ^ 1)
    early = {1: beside, 2: across, 3: across_beside, 4: up, 5: up_beside}
    for k in others:
        states[k] = attend(k, early, states[k])
    across_up, up_across, up_diagonal, up_seventh, states = lax.optimization_barrier(
        (across_up, up_across, up_diagonal, up_seventh, states)
    )
    across_up_beside = hop(across_up, sends=lambda i: i & 2 == 0, target=lambda i: i ^ 1)
    up_across_beside = hop(up_across, sends=lambda i: i & 2 > 0, target=lambda i: i ^ 1)
    up_diagonal_beside = hop(up_diagonal, sends=lambda i: i & 2 == 0, target=lambda i: i ^ 1)
    late = {
        6: across_up,
        7: across_up_beside,
        8: up_across,
        9: up_across_beside,
        10: up_seventh,
        11: up_diagonal,
        12: up_diagonal_beside,
    }

    received = []
    for k in others:
        attended, partial = attend(k, late, states[k], chunk)
        route = [(i, (i + k) % n_head) for i in range(n_head)]
        begun = lax.ppermute(partial, "head", route)
        partials = project(attended, out_weight, chunk, chunk, 2, tile)
        received.append([begun] + [lax.ppermute(partial, "head", route) for partial in partials])

    states, attended = lax.optimization_barrier((states, attended))
    attended, kept = attend(0, {**early, **late}, states[0], 2 * chunk)
    (kept_end,) = project(attended, out_weight, 2 * chunk, chunk, 1, tile)
    out = None
    for c in range(3):
        parts = [got[c] for got in received]
        at = (kept, c * chunk) if c < 2 else (kept_end, 0)
        out = combine(places[0], noise_step, gate_table, residual, *at, parts, c * chunk, chunk, tile, out)
    return out


def solution(mesh):
    in_specs = (
        P("span", "head"),
        P("span", "head"),
        P("span", "head"),
        P("head", None),
        P(("span", "head"), None),
        P(),
        P(),
        P(),
    )
    out_specs = P(("span", "head"), None)
    return jax.shard_map(
        on_device, mesh=mesh, in_specs=in_specs, out_specs=out_specs, check_vma=False
    )
```

time: 204 us -> 174 us (0.85)
  the two profiles are of different devices: /device:TPU:16 before, /device:TPU:17 now
where the time goes in v2:
time: 174 us
  Pallas kernels  121 us (70%)
  starting transfers between devices  27 us (16%)
  waiting for transfers between devices  18.1 us (10%)
  local copies, waits for them, and re-layouts  6.79 us (4%)
    pallas_call x5, Pallas kernels, attention(): pl.pallas_call(functools.partial(attention_kernel, slots, rows, group, fi...  96.7 us
    ppermute x12, starting transfers between devices, move(): return lax.ppermute(block, 'span', route)  24.2 us
    pallas_call x2, Pallas kernels, project(): pl.pallas_call(functools.partial(project_kernel, steps), out_shape=[jax.S...  18.4 us
    ppermute x12, waiting for transfers between devices, move(): return lax.ppermute(block, 'span', route)  18.1 us
    pallas_call x3, Pallas kernels, combine(): pl.pallas_call(functools.partial(combine_kernel, 1 + len(parts)), out_sha...  6.21 us
    unnamed x38, local copies, waits for them, and re-layouts  4.9 us
  transfers between devices with their start and end apart: 15, of which 5 were waited for; matrix products, arithmetic and copies ran while one was open for 0% of the time, Pallas kernels for 55%

profile of v2, /device:TPU:17, one launch (start us, length us, event | category | flops | bytes accessed | tf_op | source)
XLA Modules:
  0.0 174.3 jit_solution(5097438564377312255)
XLA Ops:
  0.0 1.2 reshape.3
  2.0 1.3 collective-permute-start.2
  3.3 1.3 collective-permute-start.1
  4.7 3.2 %collective-permute-start = (bf16[2,512,512]{2,1,0:T(8,128)(2,1)S(1)}, bf16[2,512,512]{2,1,0:T(8,128)(2,1)}, u32[]{:S(2)}, u32[]{:S(2)}) collective-permute-start(bf16[2,512,512]{2,1,0:T(8,128)(2,1)S(1)} %pad_maximum_fusion.rest_0_), channel_id=1, source_target_pairs={{0,8},{2,10},{4,12},{6,14},{8,16},{10,18},{12,20},{14,22},{16,24},... | collective-permute-start | bytes 3145736 | tf_op jit(solution)/shard_map/ppermute | solution.py:310
  8.5 9.2 %shard_map.83 = (f32[4,128,1536]{2,1,0:T(8,128)}, f32[4,8,1536]{2,1,0:T(8,128)}) custom-call(s32[2]{0:T(128)} %get-tuple-element.64.place, s32[16]{0:T(128)} %older_count.9, bf16[512,3072]{1,0:T(8,128)(2,1)} %q_ref.9, bf16[2,512,512]{2,1,0:T(8,128)(2,1)} %copy-done.7), custom_call_target="tpu_custom_call" | custom-call | tf_op jit(solution)/shard_map/pallas_call | solution.py:235
  17.7 9.2 %shard_map.82 = (f32[4,128,1536]{2,1,0:T(8,128)}, f32[4,8,1536]{2,1,0:T(8,128)}) custom-call(s32[2]{0:T(128)} %get-tuple-element.63.place, s32[16]{0:T(128)} %older_count.9, bf16[512,3072]{1,0:T(8,128)(2,1)} %q_ref.9, bf16[2,512,512]{2,1,0:T(8,128)(2,1)} %copy-done.7), custom_call_target="tpu_custom_call" | custom-call | tf_op jit(solution)/shard_map/pallas_call | solution.py:235
  27.0 2.8 %collective-permute-done.rest_3_ = bf16[2,512,512]{2,1,0:T(8,128)(2,1)} collective-permute-done((bf16[2,512,512]{2,1,0:T(8,128)(2,1)S(1)}, bf16[2,512,512]{2,1,0:T(8,128)(2,1)}, u32[]{:S(2)}, u32[]{:S(2)}) %collective-permute-start) | collective-permute-done | bytes 1048608 | tf_op jit(solution)/shard_map/ppermute | solution.py:310
  30.5 2.5 %collective-permute-start.4 = (bf16[2,512,512]{2,1,0:T(8,128)(2,1)}, bf16[2,512,512]{2,1,0:T(8,128)(2,1)S(1)}, u32[]{:S(2)}, u32[]{:S(2)}) collective-permute-start(bf16[2,512,512]{2,1,0:T(8,128)(2,1)} %collective-permute-done.rest_3_), channel_id=1, source_target_pairs={{0,2},{2,0},{4,6},{6,4},{8,10},{10,8},{12,14},{14,12},{16,18},{18,... | collective-permute-start | bytes 3145736 | tf_op jit(solution)/shard_map/ppermute | solution.py:310
  33.0 3.2 %collective-permute-start.5 = (bf16[2,512,512]{2,1,0:T(8,128)(2,1)S(1)}, bf16[2,512,512]{2,1,0:T(8,128)(2,1)S(1)}, u32[]{:S(2)}, u32[]{:S(2)}) collective-permute-start(bf16[2,512,512]{2,1,0:T(8,128)(2,1)S(1)} %collective-permute-done.1.rest_1_), channel_id=1, source_target_pairs={{0,8},{2,10},{8,16},{10,18},{16,24},{18,26},{1,9},{3,11},{9,17},{1... | collective-permute-start | bytes 3145736 | tf_op jit(solution)/shard_map/ppermute | solution.py:310
  36.2 1.4 collective-permute-start.8
  37.6 1.3 collective-permute-start.7
  38.9 4.2 %collective-permute-start.6 = (bf16[2,512,512]{2,1,0:T(8,128)(2,1)}, bf16[2,512,512]{2,1,0:T(8,128)(2,1)}, u32[]{:S(2)}, u32[]{:S(2)}) collective-permute-start(bf16[2,512,512]{2,1,0:T(8,128)(2,1)} %collective-permute-done.rest_3_), channel_id=1, source_target_pairs={{0,4},{2,6},{8,12},{10,14},{16,20},{18,22},{24,28},{26,30},{1,5},{... | collective-permute-start | bytes 3145736 | tf_op jit(solution)/shard_map/ppermute | solution.py:310
  43.1 1.0 copy-done.11
  44.1 16.2 %shard_map.84 = (f32[4,128,1536]{2,1,0:T(8,128)}, f32[4,8,1536]{2,1,0:T(8,128)}) custom-call(s32[2]{0:T(128)} %get-tuple-element.64.place, s32[16]{0:T(128)} %older_count.9, bf16[512,3072]{1,0:T(8,128)(2,1)} %q_ref.9, bf16[2,512,512]{2,1,0:T(8,128)(2,1)} %copy-done.8, bf16[2,512,512]{2,1,0:T(8,128)(2,1)} %copy-done.9, bf16[2,512,512]{2,1,0:T(8,128)(2,1)} %copy-done.10, ...), custom_call_target="tpu_custom_call" | custom-call | tf_op jit(solution)/shard_map/pallas_call | solution.py:235
  60.4 10.1 %collective-permute-done.8.rest_4_.rest_9_ = bf16[2,512,512]{2,1,0:T(8,128)(2,1)S(1)} collective-permute-done((bf16[2,512,512]{2,1,0:T(8,128)(2,1)}, bf16[2,512,512]{2,1,0:T(8,128)(2,1)S(1)}, u32[]{:S(2)}, u32[]{:S(2)}) %collective-permute-start.8) | collective-permute-done | bytes 1048608 | tf_op jit(solution)/shard_map/ppermute | solution.py:310
  70.5 3.0 %collective-permute-done.7.rest_5_.rest_10_ = bf16[2,512,512]{2,1,0:T(8,128)(2,1)S(1)} collective-permute-done((bf16[2,512,512]{2,1,0:T(8,128)(2,1)}, bf16[2,512,512]{2,1,0:T(8,128)(2,1)S(1)}, u32[]{:S(2)}, u32[]{:S(2)}) %collective-permute-start.7) | collective-permute-done | bytes 1048608 | tf_op jit(solution)/shard_map/ppermute | solution.py:310
  73.5 1.9 %collective-permute-start.9 = (bf16[2,512,512]{2,1,0:T(8,128)(2,1)S(1)}, bf16[2,512,512]{2,1,0:T(8,128)(2,1)S(1)}, u32[]{:S(2)}, u32[]{:S(2)}) collective-permute-start(bf16[2,512,512]{2,1,0:T(8,128)(2,1)S(1)} %collective-permute-done.5.rest_0_.rest_5_), channel_id=1, source_target_pairs={{0,2},{2,0},{8,10},{10,8},{16,18},{18,16},{24,26},{26,24},{1,3},{3... | collective-permute-start | bytes 3145736 | tf_op jit(solution)/shard_map/ppermute | solution.py:310
  75.4 0.7 collective-permute-start.10
  76.1 2.6 %collective-permute-start.11 = (bf16[2,512,512]{2,1,0:T(8,128)(2,1)S(1)}, bf16[2,512,512]{2,1,0:T(8,128)(2,1)S(1)}, u32[]{:S(2)}, u32[]{:S(2)}) collective-permute-start(bf16[2,512,512]{2,1,0:T(8,128)(2,1)S(1)} %collective-permute-done.7.rest_5_.rest_10_), channel_id=1, source_target_pairs={{0,2},{2,0},{8,10},{10,8},{16,18},{18,16},{24,26},{26,24},{1,3},{3... | collective-permute-start | bytes 3145736 | tf_op jit(solution)/shard_map/ppermute | solution.py:310
  78.8 2.0 %collective-permute-done.11.rest_6_.rest_11_ = bf16[2,512,512]{2,1,0:T(8,128)(2,1)S(1)} collective-permute-done((bf16[2,512,512]{2,1,0:T(8,128)(2,1)S(1)}, bf16[2,512,512]{2,1,0:T(8,128)(2,1)S(1)}, u32[]{:S(2)}, u32[]{:S(2)}) %collective-permute-start.11) | collective-permute-done | bytes 1048608 | tf_op jit(solution)/shard_map/ppermute | solution.py:310
  80.8 1.0 copy-done.17
  81.9 23.8 %shard_map.85 = (bf16[256,3072]{1,0:T(8,128)(2,1)}, bf16[256,2048]{1,0:T(8,128)(2,1)}) custom-call(s32[2]{0:T(128)} %get-tuple-element.64.place, s32[16]{0:T(128)} %older_count.9, bf16[512,3072]{1,0:T(8,128)(2,1)} %q_ref.9, bf16[2,512,512]{2,1,0:T(8,128)(2,1)} %copy-done.12, bf16[2,512,512]{2,1,0:T(8,128)(2,1)} %copy-done.15, ...), custom_call_target="tpu_custom_call" | custom-call | tf_op jit(solution)/shard_map/pallas_call | solution.py:235
  105.7 1.3 collective-permute-start.14
  107.0 1.4 copy-done.4
  108.4 11.6 %shard_map.88 = (bf16[256,2048]{1,0:T(8,128)(2,1)S(1)}, bf16[256,2048]{1,0:T(8,128)(2,1)S(1)}) custom-call(bf16[256,3072]{1,0:T(8,128)(2,1)S(1)} %copy-done.4, bf16[3072,6144]{1,0:T(8,128)(2,1)} %w_ref.3), custom_call_target="tpu_custom_call" | custom-call | tf_op jit(solution)/shard_map/pallas_call | solution.py:262
  120.3 1.2 collective-permute-start.12
  121.5 38.3 %shard_map.86 = (bf16[256,3072]{1,0:T(8,128)(2,1)}, bf16[256,4096]{1,0:T(8,128)(2,1)}) custom-call(s32[2]{0:T(128)} %get-tuple-element.63.place, s32[16]{0:T(128)} %older_count.9, bf16[512,3072]{1,0:T(8,128)(2,1)} %q_ref.9, bf16[2,512,512]{2,1,0:T(8,128)(2,1)} %copy-done.8, bf16[2,512,512]{2,1,0:T(8,128)(2,1)} %copy-done.9, bf16[2,512,512]{2,1,0:T(8,128)(2,1)} %copy-done.10, ...), custom_call_target="tpu_custom_call" | custom-call | tf_op jit(solution)/shard_map/pallas_call | solution.py:235
  159.8 1.4 copy-done.3
  161.2 6.8 %shard_map.87.rest_0_ = bf16[256,2048]{1,0:T(8,128)(2,1)S(1)} custom-call(bf16[256,3072]{1,0:T(8,128)(2,1)S(1)} %copy-done.3, bf16[3072,6144]{1,0:T(8,128)(2,1)} %w_ref.3), custom_call_target="tpu_custom_call" | custom-call | tf_op jit(solution)/shard_map/pallas_call | solution.py:262
  168.1 2.1 %shard_map.89.rest_2_ = bf16[256,6144]{1,0:T(8,128)(2,1)} custom-call(s32[2]{0:T(128)S(1)} %copy-done.5, s32[16]{0:T(128)S(1)} %copy-done.6, f32[32,6144]{1,0:T(8,128)S(1)} %copy-done.2, bf16[256,6144]{1,0:T(8,128)(2,1)S(1)} %copy-done, bf16[256,4096]{1,0:T(8,128)(2,1)S(1)} %copy-done.1, bf16[256,2048]{1,0:T(8,128)(2,1)S(1)} %collective-permute-done.14.rest_1_), custom_call_target="tpu_custom_call" | custom-call | tf_op jit(solution)/shard_map/pallas_call | solution.py:297
  170.1 2.1 %shard_map.90.rest_2_ = bf16[256,6144]{1,0:T(8,128)(2,1)} custom-call(s32[2]{0:T(128)S(1)} %copy-done.5, s32[16]{0:T(128)S(1)} %copy-done.6, f32[32,6144]{1,0:T(8,128)S(1)} %copy-done.2, bf16[256,6144]{1,0:T(8,128)(2,1)S(1)} %copy-done, bf16[256,4096]{1,0:T(8,128)(2,1)S(1)} %copy-done.1, ...), custom_call_target="tpu_custom_call", output_to_operand_aliasing={{}: (6, {})} | custom-call | tf_op jit(solution)/shard_map/pallas_call | solution.py:297
  172.2 2.1 %shard_map.91 = bf16[256,6144]{1,0:T(8,128)(2,1)} custom-call(s32[2]{0:T(128)S(1)} %copy-done.5, s32[16]{0:T(128)S(1)} %copy-done.6, f32[32,6144]{1,0:T(8,128)S(1)} %copy-done.2, bf16[256,6144]{1,0:T(8,128)(2,1)S(1)} %copy-done, bf16[256,2048]{1,0:T(8,128)(2,1)S(1)} %shard_map.87.rest_0_, ...), custom_call_target="tpu_custom_call", output_to_operand_aliasing={{}: (6, {})} | custom-call | tf_op jit(solution)/shard_map/pallas_call | solution.py:297
  (51 shorter events, 2.6 us)
Async XLA Ops:
  0.0 1.9 %copy-start.18 = (bf16[512,512]{1,0:T(8,128)(2,1)S(1)}, bf16[512,512]{1,0:T(8,128)(2,1)}, u32[]{:S(2)}) copy-start(bf16[512,512]{1,0:T(8,128)(2,1)} %param.9) | copy-start | bytes 1572868
  2.0 6.5 %copy-start.7 = (bf16[2,512,512]{2,1,0:T(8,128)(2,1)}, bf16[2,512,512]{2,1,0:T(8,128)(2,1)S(1)}, u32[]{:S(2)}) copy-start(bf16[2,512,512]{2,1,0:T(8,128)(2,1)S(1)} %pad_maximum_fusion.rest_0_) | copy-start | bytes 3145732
  2.0 24.8 %collective-permute-start.2 = (bf16[2,512,512]{2,1,0:T(8,128)(2,1)S(1)}, bf16[2,512,512]{2,1,0:T(8,128)(2,1)S(1)}, u32[]{:S(2)}, u32[]{:S(2)}) collective-permute-start(bf16[2,512,512]{2,1,0:T(8,128)(2,1)S(1)} %pad_maximum_fusion.rest_0_), channel_id=1, source_target_pairs={{0,2},{4,6},{8,10},{12,14},{16,18},{20,22},{24,26},{28,30},{1,3},{... | collective-permute-start | bytes 3145736 | tf_op jit(solution)/shard_map/ppermute | solution.py:310
  3.3 23.6 %collective-permute-start.1 = (bf16[2,512,512]{2,1,0:T(8,128)(2,1)S(1)}, bf16[2,512,512]{2,1,0:T(8,128)(2,1)S(1)}, u32[]{:S(2)}, u32[]{:S(2)}) collective-permute-start(bf16[2,512,512]{2,1,0:T(8,128)(2,1)S(1)} %pad_maximum_fusion.rest_0_), channel_id=1, source_target_pairs={{0,4},{2,6},{4,0},{6,2},{8,12},{10,14},{12,8},{14,10},{16,20},{18,... | collective-permute-start | bytes 3145736 | tf_op jit(solution)/shard_map/ppermute | solution.py:310
  4.7 25.2 %collective-permute-start = (bf16[2,512,512]{2,1,0:T(8,128)(2,1)S(1)}, bf16[2,512,512]{2,1,0:T(8,128)(2,1)}, u32[]{:S(2)}, u32[]{:S(2)}) collective-permute-start(bf16[2,512,512]{2,1,0:T(8,128)(2,1)S(1)} %pad_maximum_fusion.rest_0_), channel_id=1, source_target_pairs={{0,8},{2,10},{4,12},{6,14},{8,16},{10,18},{12,20},{14,22},{16,24},... | collective-permute-start | bytes 3145736 | tf_op jit(solution)/shard_map/ppermute | solution.py:310
  26.9 16.2 %copy-start.8 = (bf16[2,512,512]{2,1,0:T(8,128)(2,1)}, bf16[2,512,512]{2,1,0:T(8,128)(2,1)S(1)}, u32[]{:S(2)}) copy-start(bf16[2,512,512]{2,1,0:T(8,128)(2,1)S(1)} %collective-permute-done.2.rest_0_) | copy-start | bytes 3145732
  27.0 16.1 %copy-start.9 = (bf16[2,512,512]{2,1,0:T(8,128)(2,1)}, bf16[2,512,512]{2,1,0:T(8,128)(2,1)S(1)}, u32[]{:S(2)}) copy-start(bf16[2,512,512]{2,1,0:T(8,128)(2,1)S(1)} %collective-permute-done.1.rest_1_) | copy-start | bytes 3145732
  29.8 9.0 %collective-permute-start.3 = (bf16[2,512,512]{2,1,0:T(8,128)(2,1)S(1)}, bf16[2,512,512]{2,1,0:T(8,128)(2,1)S(1)}, u32[]{:S(2)}, u32[]{:S(2)}) collective-permute-start(bf16[2,512,512]{2,1,0:T(8,128)(2,1)S(1)} %collective-permute-done.1.rest_1_), channel_id=1, source_target_pairs={{4,6},{6,4},{12,14},{14,12},{20,22},{22,20},{28,30},{30,28},{5,7},... | collective-permute-start | bytes 3145736 | tf_op jit(solution)/shard_map/ppermute | solution.py:310
  30.5 12.5 %collective-permute-start.4 = (bf16[2,512,512]{2,1,0:T(8,128)(2,1)}, bf16[2,512,512]{2,1,0:T(8,128)(2,1)S(1)}, u32[]{:S(2)}, u32[]{:S(2)}) collective-permute-start(bf16[2,512,512]{2,1,0:T(8,128)(2,1)} %collective-permute-done.rest_3_), channel_id=1, source_target_pairs={{0,2},{2,0},{4,6},{6,4},{8,10},{10,8},{12,14},{14,12},{16,18},{18,... | collective-permute-start | bytes 3145736 | tf_op jit(solution)/shard_map/ppermute | solution.py:310
  33.0 27.3 %collective-permute-start.5 = (bf16[2,512,512]{2,1,0:T(8,128)(2,1)S(1)}, bf16[2,512,512]{2,1,0:T(8,128)(2,1)S(1)}, u32[]{:S(2)}, u32[]{:S(2)}) collective-permute-start(bf16[2,512,512]{2,1,0:T(8,128)(2,1)S(1)} %collective-permute-done.1.rest_1_), channel_id=1, source_target_pairs={{0,8},{2,10},{8,16},{10,18},{16,24},{18,26},{1,9},{3,11},{9,17},{1... | collective-permute-start | bytes 3145736 | tf_op jit(solution)/shard_map/ppermute | solution.py:310
  36.2 34.3 %collective-permute-start.8 = (bf16[2,512,512]{2,1,0:T(8,128)(2,1)}, bf16[2,512,512]{2,1,0:T(8,128)(2,1)S(1)}, u32[]{:S(2)}, u32[]{:S(2)}) collective-permute-start(bf16[2,512,512]{2,1,0:T(8,128)(2,1)} %collective-permute-done.rest_3_), channel_id=1, source_target_pairs={{2,8},{6,12},{10,16},{14,20},{18,24},{22,28},{3,9},{7,13},{11,17},... | collective-permute-start | bytes 3145736 | tf_op jit(solution)/shard_map/ppermute | solution.py:310
  37.6 35.9 %collective-permute-start.7 = (bf16[2,512,512]{2,1,0:T(8,128)(2,1)}, bf16[2,512,512]{2,1,0:T(8,128)(2,1)S(1)}, u32[]{:S(2)}, u32[]{:S(2)}) collective-permute-start(bf16[2,512,512]{2,1,0:T(8,128)(2,1)} %collective-permute-done.rest_3_), channel_id=1, source_target_pairs={{4,8},{6,10},{12,16},{14,18},{20,24},{22,26},{5,9},{7,11},{13,17},... | collective-permute-start | bytes 3145736 | tf_op jit(solution)/shard_map/ppermute | solution.py:310
  38.9 4.2 %copy-start.10 = (bf16[2,512,512]{2,1,0:T(8,128)(2,1)}, bf16[2,512,512]{2,1,0:T(8,128)(2,1)S(1)}, u32[]{:S(2)}) copy-start(bf16[2,512,512]{2,1,0:T(8,128)(2,1)S(1)} %collective-permute-done.3.rest_2_) | copy-start | bytes 3145732
  38.9 34.6 %collective-permute-start.6 = (bf16[2,512,512]{2,1,0:T(8,128)(2,1)}, bf16[2,512,512]{2,1,0:T(8,128)(2,1)}, u32[]{:S(2)}, u32[]{:S(2)}) collective-permute-start(bf16[2,512,512]{2,1,0:T(8,128)(2,1)} %collective-permute-done.rest_3_), channel_id=1, source_target_pairs={{0,4},{2,6},{8,12},{10,14},{16,20},{18,22},{24,28},{26,30},{1,5},{... | collective-permute-start | bytes 3145736 | tf_op jit(solution)/shard_map/ppermute | solution.py:310
  60.4 20.5 %copy-start.12 = (bf16[2,512,512]{2,1,0:T(8,128)(2,1)}, bf16[2,512,512]{2,1,0:T(8,128)(2,1)S(1)}, u32[]{:S(2)}) copy-start(bf16[2,512,512]{2,1,0:T(8,128)(2,1)S(1)} %collective-permute-done.5.rest_0_.rest_5_) | copy-start | bytes 3145732
  70.5 10.3 %copy-start.13 = (bf16[2,512,512]{2,1,0:T(8,128)(2,1)}, bf16[2,512,512]{2,1,0:T(8,128)(2,1)S(1)}, u32[]{:S(2)}) copy-start(bf16[2,512,512]{2,1,0:T(8,128)(2,1)S(1)} %collective-permute-done.8.rest_4_.rest_9_) | copy-start | bytes 3145732
  73.5 7.3 %copy-start.14 = (bf16[2,512,512]{2,1,0:T(8,128)(2,1)}, bf16[2,512,512]{2,1,0:T(8,128)(2,1)S(1)}, u32[]{:S(2)}) copy-start(bf16[2,512,512]{2,1,0:T(8,128)(2,1)S(1)} %collective-permute-done.7.rest_5_.rest_10_) | copy-start | bytes 3145732
  73.5 5.3 %collective-permute-start.9 = (bf16[2,512,512]{2,1,0:T(8,128)(2,1)S(1)}, bf16[2,512,512]{2,1,0:T(8,128)(2,1)S(1)}, u32[]{:S(2)}, u32[]{:S(2)}) collective-permute-start(bf16[2,512,512]{2,1,0:T(8,128)(2,1)S(1)} %collective-permute-done.5.rest_0_.rest_5_), channel_id=1, source_target_pairs={{0,2},{2,0},{8,10},{10,8},{16,18},{18,16},{24,26},{26,24},{1,3},{3... | collective-permute-start | bytes 3145736 | tf_op jit(solution)/shard_map/ppermute | solution.py:310
  75.4 3.4 %collective-permute-start.10 = (bf16[2,512,512]{2,1,0:T(8,128)(2,1)}, bf16[2,512,512]{2,1,0:T(8,128)(2,1)S(1)}, u32[]{:S(2)}, u32[]{:S(2)}) collective-permute-start(bf16[2,512,512]{2,1,0:T(8,128)(2,1)} %collective-permute-done.6.rest_2_.rest_7_), channel_id=1, source_target_pairs={{4,6},{6,4},{12,14},{14,12},{20,22},{22,20},{28,30},{30,28},{5,7},... | collective-permute-start | bytes 3145736 | tf_op jit(solution)/shard_map/ppermute | solution.py:310
  76.1 4.7 %collective-permute-start.11 = (bf16[2,512,512]{2,1,0:T(8,128)(2,1)S(1)}, bf16[2,512,512]{2,1,0:T(8,128)(2,1)S(1)}, u32[]{:S(2)}, u32[]{:S(2)}) collective-permute-start(bf16[2,512,512]{2,1,0:T(8,128)(2,1)S(1)} %collective-permute-done.7.rest_5_.rest_10_), channel_id=1, source_target_pairs={{0,2},{2,0},{8,10},{10,8},{16,18},{18,16},{24,26},{26,24},{1,3},{3... | collective-permute-start | bytes 3145736 | tf_op jit(solution)/shard_map/ppermute | solution.py:310
  78.7 2.1 %copy-start.15 = (bf16[2,512,512]{2,1,0:T(8,128)(2,1)}, bf16[2,512,512]{2,1,0:T(8,128)(2,1)S(1)}, u32[]{:S(2)}) copy-start(bf16[2,512,512]{2,1,0:T(8,128)(2,1)S(1)} %collective-permute-done.9.rest_1_.rest_6_) | copy-start | bytes 3145732
  78.8 2.1 %copy-start.16 = (bf16[2,512,512]{2,1,0:T(8,128)(2,1)}, bf16[2,512,512]{2,1,0:T(8,128)(2,1)S(1)}, u32[]{:S(2)}) copy-start(bf16[2,512,512]{2,1,0:T(8,128)(2,1)S(1)} %collective-permute-done.10.rest_3_.rest_8_) | copy-start | bytes 3145732
  105.7 62.3 %collective-permute-start.14 = (bf16[256,2048]{1,0:T(8,128)(2,1)}, bf16[256,2048]{1,0:T(8,128)(2,1)S(1)}, u32[]{:S(2)}, u32[]{:S(2)}) collective-permute-start(bf16[256,2048]{1,0:T(8,128)(2,1)} %get-tuple-element.62), channel_id=1, source_target_pairs={{0,1},{1,0},{2,3},{3,2},{4,5},{5,4},{6,7},{7,6},{8,9},{9,8},{10,11... | collective-permute-start | bytes 3145736 | tf_op jit(solution)/shard_map/ppermute | solution.py:380
  107.0 1.4 copy-start.4
  120.0 50.2 %collective-permute-start.13 = (bf16[256,2048]{1,0:T(8,128)(2,1)S(1)}, bf16[256,2048]{1,0:T(8,128)(2,1)S(1)}, u32[]{:S(2)}, u32[]{:S(2)}) collective-permute-start(bf16[256,2048]{1,0:T(8,128)(2,1)S(1)} %get-tuple-element.61), channel_id=1, source_target_pairs={{0,1},{1,0},{2,3},{3,2},{4,5},{5,4},{6,7},{7,6},{8,9},{9,8},{10,11... | collective-permute-start | bytes 3145736 | tf_op jit(solution)/shard_map/ppermute | solution.py:382
  120.3 51.9 %collective-permute-start.12 = (bf16[256,2048]{1,0:T(8,128)(2,1)S(1)}, bf16[256,2048]{1,0:T(8,128)(2,1)S(1)}, u32[]{:S(2)}, u32[]{:S(2)}) collective-permute-start(bf16[256,2048]{1,0:T(8,128)(2,1)S(1)} %get-tuple-element.59), channel_id=1, source_target_pairs={{0,1},{1,0},{2,3},{3,2},{4,5},{5,4},{6,7},{7,6},{8,9},{9,8},{10,11... | collective-permute-start | bytes 3145736 | tf_op jit(solution)/shard_map/ppermute | solution.py:382
  159.8 1.4 copy-start.3
  161.2 6.8 %copy-start = (bf16[256,6144]{1,0:T(8,128)(2,1)S(1)}, bf16[256,6144]{1,0:T(8,128)(2,1)}, u32[]{:S(2)}) copy-start(bf16[256,6144]{1,0:T(8,128)(2,1)} %residual_ref.5) | copy-start | bytes 9437188
  161.2 6.8 %copy-start.1 = (bf16[256,4096]{1,0:T(8,128)(2,1)S(1)}, bf16[256,4096]{1,0:T(8,128)(2,1)}, u32[]{:S(2)}) copy-start(bf16[256,4096]{1,0:T(8,128)(2,1)} %get-tuple-element.60.rest_0_) | copy-start | bytes 6291460
  161.2 6.8 %copy-start.2 = (f32[32,6144]{1,0:T(8,128)S(1)}, f32[32,6144]{1,0:T(8,128)}, u32[]{:S(2)}) copy-start(f32[32,6144]{1,0:T(8,128)} %gate_ref.5) | copy-start | bytes 2359300
  161.2 6.8 %copy-start.5 = (s32[2]{0:T(128)S(1)}, s32[2]{0:T(128)}, u32[]{:S(2)}) copy-start(s32[2]{0:T(128)} %get-tuple-element.63.place) | copy-start | bytes 28
  161.2 6.8 %copy-start.6 = (s32[16]{0:T(128)S(1)}, s32[16]{0:T(128)}, u32[]{:S(2)}) copy-start(s32[16]{0:T(128)} %noise_step.5) | copy-start | bytes 196
  (2 other events, 2.0 us)

commit v3 on v2

--- a/solution.py
+++ b/solution.py
@@ -12,6 +12,8 @@
 MAX_BLOCKS = 8
 EXPONENT_SCALE = math.log2(math.e) / math.sqrt(HEAD_SIZE)
 TOTAL_LIMIT = 2.0**100
+EARLY = (1, 2, 3, 4, 5)
+EARLY_LIMIT = 5
 F32 = jnp.float32
 BF16 = jnp.bfloat16
 
@@ -36,7 +38,7 @@
     ][slot]
 
 
-def attention_kernel(slots, rows, group, first, last, place, older_count, q_ref, *rest):
+def attention_kernel(slots, rows, group, first, last, share, place, older_count, q_ref, *rest):
     kv_refs, rest = rest[: len(slots)], rest[len(slots) :]
     if not first:
         (sum_in, mark_in), rest = rest[:2], rest[2:]
@@ -52,14 +54,25 @@
     my_span = place[1]
     older_mine = older_count[my_span]
 
+    def in_view(slot):
+        source, used = slot_source(slot, my_span)
+        return used & (source <= my_span) & (my_span - source <= older_mine)
+
+    def number(flags):
+        return sum(jnp.where(flag, 1, 0).astype(jnp.int32) for flag in flags)
+
+    views = [in_view(slot) for slot in slots]
+    if share:
+        earlies = [in_view(slot) for slot in EARLY]
+        n_early = number(earlies)
+        first_part = jnp.maximum(EARLY_LIMIT - n_early, 0)
+        for n, slot in enumerate(EARLY):
+            before = number(earlies[:n]) if n else 0
+            taken = before < first_part
+            views[slots.index(slot)] = earlies[n] & (taken if share == "begin" else jnp.logical_not(taken))
     places = []
     count = jnp.int32(0)
-    for slot in slots:
-        if slot == 0:
-            seen = my_span >= 0
-        else:
-            source, used = slot_source(slot, my_span)
-            seen = used & (source < my_span) & (my_span - source <= older_mine)
+    for seen in views:
         places.append((seen, count))
         count = count + jnp.where(seen, 1, 0).astype(jnp.int32)
 
@@ -185,7 +198,7 @@
             product_ref[:, at] = product.astype(BF16)
 
 
-def attention(queries, place, older_count, rows, group, blocks, state=None, weight=None, columns=0):
+def attention(queries, place, older_count, rows, group, blocks, state=None, weight=None, columns=0, share=""):
     slots = sorted(blocks)
     arrays = [blocks[slot] for slot in slots]
     first = state is None
@@ -201,7 +214,7 @@
     ]
     high = HEAD_SIZE + 16
     in_specs = [pl.BlockSpec((rows, width), lambda g, p, o: (p[0], g))]
-    in_specs += [pl.BlockSpec(memory_space=pltpu.HBM)] * len(arrays)
+    in_specs += [pl.BlockSpec(memory_space=pl.ANY)] * len(arrays)
     scratch = [
         pltpu.VMEM((2, n_block, span, 2 * HEAD_SIZE), BF16),
         pltpu.VMEM((2, n_block, high, span), BF16),
@@ -213,11 +226,11 @@
         in_specs += state_specs
         arrays += list(state)
     if last:
-        in_specs.append(pl.BlockSpec(memory_space=pltpu.HBM))
+        in_specs.append(pl.BlockSpec(memory_space=pl.ANY))
         arrays.append(weight)
         out_shape = [
-            jax.ShapeDtypeStruct((rows, kv_heads * width), BF16),
-            jax.ShapeDtypeStruct((rows, columns), BF16),
+            pltpu.HBM((rows, kv_heads * width), BF16),
+            pltpu.HBM((rows, columns), BF16),
         ]
         out_specs = [
             pl.BlockSpec((rows, width), lambda g, p, o: (0, g)),
@@ -233,7 +246,7 @@
         out_shape = [pltpu.HBM((kv_heads, n, all_rows), F32) for n in (HEAD_SIZE, 8)]
         out_specs = state_specs
     return pl.pallas_call(
-        functools.partial(attention_kernel, slots, rows, group, first, last),
+        functools.partial(attention_kernel, slots, rows, group, first, last, share),
         out_shape=out_shape,
         grid_spec=pltpu.PrefetchScalarGridSpec(
             num_scalar_prefetch=2,
@@ -338,9 +351,9 @@
     tile = model_width // 6
     chunk = 2 * tile
 
-    def attend(k, blocks, state=None, columns=0):
+    def attend(k, blocks, state=None, columns=0, share=""):
         weight = out_weight if columns else None
-        return attention(queries, places[k], older_count, rows, group, blocks, state, weight, columns)
+        return attention(queries, places[k], older_count, rows, group, blocks, state, weight, columns, share)
 
     others = range(1, n_head)
     up = hop(own, sends=lambda i: True, target=lambda i: i + 4)
@@ -357,6 +370,7 @@
     early = {1: beside, 2: across, 3: across_beside, 4: up, 5: up_beside}
     for k in others:
         states[k] = attend(k, early, states[k])
+    states[0] = attend(0, early, states[0], share="begin")
     across_up, up_across, up_diagonal, up_seventh, states = lax.optimization_barrier(
         (across_up, up_across, up_diagonal, up_seventh, states)
     )
@@ -382,7 +396,7 @@
         received.append([begun] + [lax.ppermute(partial, "head", route) for partial in partials])
 
     states, attended = lax.optimization_barrier((states, attended))
-    attended, kept = attend(0, {**early, **late}, states[0], 2 * chunk)
+    attended, kept = attend(0, {**early, **late}, states[0], 2 * chunk, share="end")
     (kept_end,) = project(attended, out_weight, 2 * chunk, chunk, 1, tile)
     out = None
     for c in range(3):

time: 174 us -> 175 us (level); the launches traced: 174 us -> 172 us
  Pallas kernels: 121 us -> 107 us
  waiting for transfers between devices: 18.1 us -> 29.5 us
    ppermute x2, waiting for transfers between devices: 0.01 us -> 15.4 us  [on_device(): lax.ppermute(partial, 'head', route)]
    pallas_call x5 -> x6, Pallas kernels: 96.7 us -> 82.3 us  [attention(): pl.pallas_call(functools.partial(attention_kernel, slots, rows, group, fi...]
    ppermute x12, waiting for transfers between devices: 18.1 us -> 14.1 us  [move(): return lax.ppermute(block, 'span', route)]
    unnamed x38 -> x36, local copies, waits for them, and re-layouts: 4.9 us -> 4.81 us
  transfers between devices with their start and end apart: 15 -> 15, of which waited for: 5 -> 6; matrix products, arithmetic and copies ran while one was open for 0% -> 0% of each run, Pallas kernels for 55% -> 51%
where the time goes in v3:
time: 175 us; the launch traced here: 172 us
  Pallas kernels  107 us (61%)
  waiting for transfers between devices  29.5 us (17%)
  starting transfers between devices  27.1 us (15%)
  local copies, waits for them, and re-layouts  6.7 us (4%)
    pallas_call x6, Pallas kernels, attention(): pl.pallas_call(functools.partial(attention_kernel, slots, rows, group, fi...  82.3 us
    ppermute x12, starting transfers between devices, move(): return lax.ppermute(block, 'span', route)  24.2 us
    pallas_call x2, Pallas kernels, project(): pl.pallas_call(functools.partial(project_kernel, steps), out_shape=[jax.S...  18.4 us
    ppermute x2, waiting for transfers between devices, on_device(): lax.ppermute(partial, 'head', route)  15.4 us
    ppermute x12, waiting for transfers between devices, move(): return lax.ppermute(block, 'span', route)  14.1 us
    pallas_call x3, Pallas kernels, combine(): pl.pallas_call(functools.partial(combine_kernel, 1 + len(parts)), out_sha...  6.21 us
    unnamed x36, local copies, waits for them, and re-layouts  4.81 us
  transfers between devices with their start and end apart: 15, of which 6 were waited for; matrix products, arithmetic and copies ran while one was open for 0% of the time, Pallas kernels for 51%

profile of v3, /device:TPU:17, one launch (start us, length us, event | category | flops | bytes accessed | tf_op | source)
XLA Modules:
  0.0 172.2 jit_solution(2366892295071997254)
XLA Ops:
  0.0 1.2 reshape.3
  1.9 1.1 pad_maximum_fusion.rest_0_
  3.0 1.3 collective-permute-start.2
  4.3 1.3 collective-permute-start.1
  5.6 3.2 %collective-permute-start = (bf16[2,512,512]{2,1,0:T(8,128)(2,1)}, bf16[2,512,512]{2,1,0:T(8,128)(2,1)}, u32[]{:S(2)}, u32[]{:S(2)}) collective-permute-start(bf16[2,512,512]{2,1,0:T(8,128)(2,1)} %pad_maximum_fusion.rest_0_), channel_id=1, source_target_pairs={{0,8},{2,10},{4,12},{6,14},{8,16},{10,18},{12,20},{14,22},{16,24},... | collective-permute-start | bytes 3145736 | tf_op jit(solution)/shard_map/ppermute | solution.py:323
  9.4 9.2 %shard_map.83 = (f32[4,128,1536]{2,1,0:T(8,128)}, f32[4,8,1536]{2,1,0:T(8,128)}) custom-call(s32[2]{0:T(128)} %get-tuple-element.68.place, s32[16]{0:T(128)} %older_count.11, bf16[512,3072]{1,0:T(8,128)(2,1)} %q_ref.11, bf16[2,512,512]{2,1,0:T(8,128)(2,1)} %pad_maximum_fusion.rest_0_), custom_call_target="tpu_custom_call" | custom-call | tf_op jit(solution)/shard_map/pallas_call | solution.py:248
  18.6 9.2 %shard_map.82 = (f32[4,128,1536]{2,1,0:T(8,128)}, f32[4,8,1536]{2,1,0:T(8,128)}) custom-call(s32[2]{0:T(128)} %get-tuple-element.67.place, s32[16]{0:T(128)} %older_count.11, bf16[512,3072]{1,0:T(8,128)(2,1)} %q_ref.11, bf16[2,512,512]{2,1,0:T(8,128)(2,1)} %pad_maximum_fusion.rest_0_), custom_call_target="tpu_custom_call" | custom-call | tf_op jit(solution)/shard_map/pallas_call | solution.py:248
  28.2 2.8 %collective-permute-done.rest_3_ = bf16[2,512,512]{2,1,0:T(8,128)(2,1)} collective-permute-done((bf16[2,512,512]{2,1,0:T(8,128)(2,1)}, bf16[2,512,512]{2,1,0:T(8,128)(2,1)}, u32[]{:S(2)}, u32[]{:S(2)}) %collective-permute-start) | collective-permute-done | bytes 1048608 | tf_op jit(solution)/shard_map/ppermute | solution.py:323
  31.7 2.5 %collective-permute-start.4 = (bf16[2,512,512]{2,1,0:T(8,128)(2,1)}, bf16[2,512,512]{2,1,0:T(8,128)(2,1)S(1)}, u32[]{:S(2)}, u32[]{:S(2)}) collective-permute-start(bf16[2,512,512]{2,1,0:T(8,128)(2,1)} %collective-permute-done.rest_3_), channel_id=1, source_target_pairs={{0,2},{2,0},{4,6},{6,4},{8,10},{10,8},{12,14},{14,12},{16,18},{18,... | collective-permute-start | bytes 3145736 | tf_op jit(solution)/shard_map/ppermute | solution.py:323
  34.2 3.2 %collective-permute-start.5 = (bf16[2,512,512]{2,1,0:T(8,128)(2,1)S(1)}, bf16[2,512,512]{2,1,0:T(8,128)(2,1)S(1)}, u32[]{:S(2)}, u32[]{:S(2)}) collective-permute-start(bf16[2,512,512]{2,1,0:T(8,128)(2,1)S(1)} %collective-permute-done.1.rest_1_), channel_id=1, source_target_pairs={{0,8},{2,10},{8,16},{10,18},{16,24},{18,26},{1,9},{3,11},{9,17},{1... | collective-permute-start | bytes 3145736 | tf_op jit(solution)/shard_map/ppermute | solution.py:323
  37.4 1.4 collective-permute-start.8
  38.7 1.3 collective-permute-start.7
  40.1 4.2 %collective-permute-start.6 = (bf16[2,512,512]{2,1,0:T(8,128)(2,1)}, bf16[2,512,512]{2,1,0:T(8,128)(2,1)}, u32[]{:S(2)}, u32[]{:S(2)}) collective-permute-start(bf16[2,512,512]{2,1,0:T(8,128)(2,1)} %collective-permute-done.rest_3_), channel_id=1, source_target_pairs={{0,4},{2,6},{8,12},{10,14},{16,20},{18,22},{24,28},{26,30},{1,5},{... | collective-permute-start | bytes 3145736 | tf_op jit(solution)/shard_map/ppermute | solution.py:323
  45.3 10.2 %shard_map.85 = (f32[4,128,1536]{2,1,0:T(8,128)}, f32[4,8,1536]{2,1,0:T(8,128)}) custom-call(s32[2]{0:T(128)} %get-tuple-element.68.place, s32[16]{0:T(128)} %older_count.11, bf16[512,3072]{1,0:T(8,128)(2,1)} %q_ref.11, bf16[2,512,512]{2,1,0:T(8,128)(2,1)} %copy-done.7, bf16[2,512,512]{2,1,0:T(8,128)(2,1)} %copy-done.8, bf16[2,512,512]{2,1,0:T(8,128)(2,1)} %copy-done.9, ...), custom_call_target="tpu_custom_call" | custom-call | tf_op jit(solution)/shard_map/pallas_call | solution.py:248
  55.5 10.2 %shard_map.84 = (f32[4,128,1536]{2,1,0:T(8,128)}, f32[4,8,1536]{2,1,0:T(8,128)}) custom-call(s32[2]{0:T(128)} %get-tuple-element.67.place, s32[16]{0:T(128)} %older_count.11, bf16[512,3072]{1,0:T(8,128)(2,1)} %q_ref.11, bf16[2,512,512]{2,1,0:T(8,128)(2,1)} %copy-done.7, bf16[2,512,512]{2,1,0:T(8,128)(2,1)} %copy-done.8, bf16[2,512,512]{2,1,0:T(8,128)(2,1)} %copy-done.9, ...), custom_call_target="tpu_custom_call" | custom-call | tf_op jit(solution)/shard_map/pallas_call | solution.py:248
  65.7 6.0 %collective-permute-done.8.rest_4_.rest_9_ = bf16[2,512,512]{2,1,0:T(8,128)(2,1)S(1)} collective-permute-done((bf16[2,512,512]{2,1,0:T(8,128)(2,1)}, bf16[2,512,512]{2,1,0:T(8,128)(2,1)S(1)}, u32[]{:S(2)}, u32[]{:S(2)}) %collective-permute-start.8) | collective-permute-done | bytes 1048608 | tf_op jit(solution)/shard_map/ppermute | solution.py:323
  71.7 3.0 %collective-permute-done.7.rest_5_.rest_10_ = bf16[2,512,512]{2,1,0:T(8,128)(2,1)S(1)} collective-permute-done((bf16[2,512,512]{2,1,0:T(8,128)(2,1)}, bf16[2,512,512]{2,1,0:T(8,128)(2,1)S(1)}, u32[]{:S(2)}, u32[]{:S(2)}) %collective-permute-start.7) | collective-permute-done | bytes 1048608 | tf_op jit(solution)/shard_map/ppermute | solution.py:323
  74.7 1.9 %collective-permute-start.9 = (bf16[2,512,512]{2,1,0:T(8,128)(2,1)S(1)}, bf16[2,512,512]{2,1,0:T(8,128)(2,1)S(1)}, u32[]{:S(2)}, u32[]{:S(2)}) collective-permute-start(bf16[2,512,512]{2,1,0:T(8,128)(2,1)S(1)} %collective-permute-done.5.rest_0_.rest_5_), channel_id=1, source_target_pairs={{0,2},{2,0},{8,10},{10,8},{16,18},{18,16},{24,26},{26,24},{1,3},{3... | collective-permute-start | bytes 3145736 | tf_op jit(solution)/shard_map/ppermute | solution.py:323
  77.3 2.6 %collective-permute-start.11 = (bf16[2,512,512]{2,1,0:T(8,128)(2,1)S(1)}, bf16[2,512,512]{2,1,0:T(8,128)(2,1)S(1)}, u32[]{:S(2)}, u32[]{:S(2)}) collective-permute-start(bf16[2,512,512]{2,1,0:T(8,128)(2,1)S(1)} %collective-permute-done.7.rest_5_.rest_10_), channel_id=1, source_target_pairs={{0,2},{2,0},{8,10},{10,8},{16,18},{18,16},{24,26},{26,24},{1,3},{3... | collective-permute-start | bytes 3145736 | tf_op jit(solution)/shard_map/ppermute | solution.py:323
  79.9 2.0 %collective-permute-done.11.rest_6_.rest_11_ = bf16[2,512,512]{2,1,0:T(8,128)(2,1)S(1)} collective-permute-done((bf16[2,512,512]{2,1,0:T(8,128)(2,1)S(1)}, bf16[2,512,512]{2,1,0:T(8,128)(2,1)S(1)}, u32[]{:S(2)}, u32[]{:S(2)}) %collective-permute-start.11) | collective-permute-done | bytes 1048608 | tf_op jit(solution)/shard_map/ppermute | solution.py:323
  83.0 17.6 %shard_map.86 = (bf16[256,3072]{1,0:T(8,128)(2,1)}, bf16[256,2048]{1,0:T(8,128)(2,1)}) custom-call(s32[2]{0:T(128)} %get-tuple-element.68.place, s32[16]{0:T(128)} %older_count.11, bf16[512,3072]{1,0:T(8,128)(2,1)} %q_ref.11, bf16[2,512,512]{2,1,0:T(8,128)(2,1)} %copy-done.11, bf16[2,512,512]{2,1,0:T(8,128)(2,1)} %copy-done.14, ...), custom_call_target="tpu_custom_call" | custom-call | tf_op jit(solution)/shard_map/pallas_call | solution.py:248
  100.6 1.3 collective-permute-start.14
  101.9 1.4 copy-done.4
  103.3 11.6 %shard_map.89 = (bf16[256,2048]{1,0:T(8,128)(2,1)S(1)}, bf16[256,2048]{1,0:T(8,128)(2,1)S(1)}) custom-call(bf16[256,3072]{1,0:T(8,128)(2,1)S(1)} %copy-done.4, bf16[3072,6144]{1,0:T(8,128)(2,1)} %w_ref.3), custom_call_target="tpu_custom_call" | custom-call | tf_op jit(solution)/shard_map/pallas_call | solution.py:275
  115.2 1.2 collective-permute-start.12
  116.4 25.9 %shard_map.87 = (bf16[256,3072]{1,0:T(8,128)(2,1)}, bf16[256,4096]{1,0:T(8,128)(2,1)}) custom-call(s32[2]{0:T(128)} %get-tuple-element.67.place, s32[16]{0:T(128)} %older_count.11, bf16[512,3072]{1,0:T(8,128)(2,1)} %q_ref.11, bf16[2,512,512]{2,1,0:T(8,128)(2,1)} %copy-done.7, bf16[2,512,512]{2,1,0:T(8,128)(2,1)} %copy-done.8, ...), custom_call_target="tpu_custom_call" | custom-call | tf_op jit(solution)/shard_map/pallas_call | solution.py:248
  142.4 1.4 copy-done.3
  143.8 6.8 %shard_map.88.rest_0_ = bf16[256,2048]{1,0:T(8,128)(2,1)S(1)} custom-call(bf16[256,3072]{1,0:T(8,128)(2,1)S(1)} %copy-done.3, bf16[3072,6144]{1,0:T(8,128)(2,1)} %w_ref.3), custom_call_target="tpu_custom_call" | custom-call | tf_op jit(solution)/shard_map/pallas_call | solution.py:275
  150.6 2.1 %shard_map.90.rest_2_ = bf16[256,6144]{1,0:T(8,128)(2,1)} custom-call(s32[2]{0:T(128)S(1)} %copy-done.5, s32[16]{0:T(128)S(1)} %copy-done.6, f32[32,6144]{1,0:T(8,128)S(1)} %copy-done.2, bf16[256,6144]{1,0:T(8,128)(2,1)S(1)} %copy-done, bf16[256,4096]{1,0:T(8,128)(2,1)S(1)} %copy-done.1, bf16[256,2048]{1,0:T(8,128)(2,1)S(1)} %collective-permute-done.14.rest_1_), custom_call_target="tpu_custom_call" | custom-call | tf_op jit(solution)/shard_map/pallas_call | solution.py:310
  152.7 2.1 %shard_map.91.rest_2_ = bf16[256,6144]{1,0:T(8,128)(2,1)} custom-call(s32[2]{0:T(128)S(1)} %copy-done.5, s32[16]{0:T(128)S(1)} %copy-done.6, f32[32,6144]{1,0:T(8,128)S(1)} %copy-done.2, bf16[256,6144]{1,0:T(8,128)(2,1)S(1)} %copy-done, bf16[256,4096]{1,0:T(8,128)(2,1)S(1)} %copy-done.1, ...), custom_call_target="tpu_custom_call", output_to_operand_aliasing={{}: (6, {})} | custom-call | tf_op jit(solution)/shard_map/pallas_call | solution.py:310
  154.8 15.4 %collective-permute-done.12.rest_1_ = bf16[256,2048]{1,0:T(8,128)(2,1)S(1)} collective-permute-done((bf16[256,2048]{1,0:T(8,128)(2,1)S(1)}, bf16[256,2048]{1,0:T(8,128)(2,1)S(1)}, u32[]{:S(2)}, u32[]{:S(2)}) %collective-permute-start.12) | collective-permute-done | bytes 1048608 | tf_op jit(solution)/shard_map/ppermute | solution.py:396
  170.1 2.1 %shard_map.92 = bf16[256,6144]{1,0:T(8,128)(2,1)} custom-call(s32[2]{0:T(128)S(1)} %copy-done.5, s32[16]{0:T(128)S(1)} %copy-done.6, f32[32,6144]{1,0:T(8,128)S(1)} %copy-done.2, bf16[256,6144]{1,0:T(8,128)(2,1)S(1)} %copy-done, bf16[256,2048]{1,0:T(8,128)(2,1)S(1)} %shard_map.88.rest_0_, ...), custom_call_target="tpu_custom_call", output_to_operand_aliasing={{}: (6, {})} | custom-call | tf_op jit(solution)/shard_map/pallas_call | solution.py:310
  (50 shorter events, 5.4 us)
Async XLA Ops:
  0.0 1.9 %copy-start.17 = (bf16[512,512]{1,0:T(8,128)(2,1)S(1)}, bf16[512,512]{1,0:T(8,128)(2,1)}, u32[]{:S(2)}) copy-start(bf16[512,512]{1,0:T(8,128)(2,1)} %param.9) | copy-start | bytes 1572868
  3.0 24.8 %collective-permute-start.2 = (bf16[2,512,512]{2,1,0:T(8,128)(2,1)}, bf16[2,512,512]{2,1,0:T(8,128)(2,1)S(1)}, u32[]{:S(2)}, u32[]{:S(2)}) collective-permute-start(bf16[2,512,512]{2,1,0:T(8,128)(2,1)} %pad_maximum_fusion.rest_0_), channel_id=1, source_target_pairs={{0,2},{4,6},{8,10},{12,14},{16,18},{20,22},{24,26},{28,30},{1,3},{... | collective-permute-start | bytes 3145736 | tf_op jit(solution)/shard_map/ppermute | solution.py:323
  4.3 23.8 %collective-permute-start.1 = (bf16[2,512,512]{2,1,0:T(8,128)(2,1)}, bf16[2,512,512]{2,1,0:T(8,128)(2,1)S(1)}, u32[]{:S(2)}, u32[]{:S(2)}) collective-permute-start(bf16[2,512,512]{2,1,0:T(8,128)(2,1)} %pad_maximum_fusion.rest_0_), channel_id=1, source_target_pairs={{0,4},{2,6},{4,0},{6,2},{8,12},{10,14},{12,8},{14,10},{16,20},{18,... | collective-permute-start | bytes 3145736 | tf_op jit(solution)/shard_map/ppermute | solution.py:323
  5.6 25.4 %collective-permute-start = (bf16[2,512,512]{2,1,0:T(8,128)(2,1)}, bf16[2,512,512]{2,1,0:T(8,128)(2,1)}, u32[]{:S(2)}, u32[]{:S(2)}) collective-permute-start(bf16[2,512,512]{2,1,0:T(8,128)(2,1)} %pad_maximum_fusion.rest_0_), channel_id=1, source_target_pairs={{0,8},{2,10},{4,12},{6,14},{8,16},{10,18},{12,20},{14,22},{16,24},... | collective-permute-start | bytes 3145736 | tf_op jit(solution)/shard_map/ppermute | solution.py:323
  27.8 16.5 %copy-start.7 = (bf16[2,512,512]{2,1,0:T(8,128)(2,1)}, bf16[2,512,512]{2,1,0:T(8,128)(2,1)S(1)}, u32[]{:S(2)}) copy-start(bf16[2,512,512]{2,1,0:T(8,128)(2,1)S(1)} %collective-permute-done.2.rest_0_) | copy-start | bytes 3145732
  28.2 16.1 %copy-start.8 = (bf16[2,512,512]{2,1,0:T(8,128)(2,1)}, bf16[2,512,512]{2,1,0:T(8,128)(2,1)S(1)}, u32[]{:S(2)}) copy-start(bf16[2,512,512]{2,1,0:T(8,128)(2,1)S(1)} %collective-permute-done.1.rest_1_) | copy-start | bytes 3145732
  31.0 9.0 %collective-permute-start.3 = (bf16[2,512,512]{2,1,0:T(8,128)(2,1)S(1)}, bf16[2,512,512]{2,1,0:T(8,128)(2,1)S(1)}, u32[]{:S(2)}, u32[]{:S(2)}) collective-permute-start(bf16[2,512,512]{2,1,0:T(8,128)(2,1)S(1)} %collective-permute-done.1.rest_1_), channel_id=1, source_target_pairs={{4,6},{6,4},{12,14},{14,12},{20,22},{22,20},{28,30},{30,28},{5,7},... | collective-permute-start | bytes 3145736 | tf_op jit(solution)/shard_map/ppermute | solution.py:323
  31.7 12.6 %collective-permute-start.4 = (bf16[2,512,512]{2,1,0:T(8,128)(2,1)}, bf16[2,512,512]{2,1,0:T(8,128)(2,1)S(1)}, u32[]{:S(2)}, u32[]{:S(2)}) collective-permute-start(bf16[2,512,512]{2,1,0:T(8,128)(2,1)} %collective-permute-done.rest_3_), channel_id=1, source_target_pairs={{0,2},{2,0},{4,6},{6,4},{8,10},{10,8},{12,14},{14,12},{16,18},{18,... | collective-permute-start | bytes 3145736 | tf_op jit(solution)/shard_map/ppermute | solution.py:323
  34.2 31.5 %collective-permute-start.5 = (bf16[2,512,512]{2,1,0:T(8,128)(2,1)S(1)}, bf16[2,512,512]{2,1,0:T(8,128)(2,1)S(1)}, u32[]{:S(2)}, u32[]{:S(2)}) collective-permute-start(bf16[2,512,512]{2,1,0:T(8,128)(2,1)S(1)} %collective-permute-done.1.rest_1_), channel_id=1, source_target_pairs={{0,8},{2,10},{8,16},{10,18},{16,24},{18,26},{1,9},{3,11},{9,17},{1... | collective-permute-start | bytes 3145736 | tf_op jit(solution)/shard_map/ppermute | solution.py:323
  37.4 34.3 %collective-permute-start.8 = (bf16[2,512,512]{2,1,0:T(8,128)(2,1)}, bf16[2,512,512]{2,1,0:T(8,128)(2,1)S(1)}, u32[]{:S(2)}, u32[]{:S(2)}) collective-permute-start(bf16[2,512,512]{2,1,0:T(8,128)(2,1)} %collective-permute-done.rest_3_), channel_id=1, source_target_pairs={{2,8},{6,12},{10,16},{14,20},{18,24},{22,28},{3,9},{7,13},{11,17},... | collective-permute-start | bytes 3145736 | tf_op jit(solution)/shard_map/ppermute | solution.py:323
  38.7 35.9 %collective-permute-start.7 = (bf16[2,512,512]{2,1,0:T(8,128)(2,1)}, bf16[2,512,512]{2,1,0:T(8,128)(2,1)S(1)}, u32[]{:S(2)}, u32[]{:S(2)}) collective-permute-start(bf16[2,512,512]{2,1,0:T(8,128)(2,1)} %collective-permute-done.rest_3_), channel_id=1, source_target_pairs={{4,8},{6,10},{12,16},{14,18},{20,24},{22,26},{5,9},{7,11},{13,17},... | collective-permute-start | bytes 3145736 | tf_op jit(solution)/shard_map/ppermute | solution.py:323
  40.1 4.3 %copy-start.9 = (bf16[2,512,512]{2,1,0:T(8,128)(2,1)}, bf16[2,512,512]{2,1,0:T(8,128)(2,1)S(1)}, u32[]{:S(2)}) copy-start(bf16[2,512,512]{2,1,0:T(8,128)(2,1)S(1)} %collective-permute-done.3.rest_2_) | copy-start | bytes 3145732
  40.1 34.6 %collective-permute-start.6 = (bf16[2,512,512]{2,1,0:T(8,128)(2,1)}, bf16[2,512,512]{2,1,0:T(8,128)(2,1)}, u32[]{:S(2)}, u32[]{:S(2)}) collective-permute-start(bf16[2,512,512]{2,1,0:T(8,128)(2,1)} %collective-permute-done.rest_3_), channel_id=1, source_target_pairs={{0,4},{2,6},{8,12},{10,14},{16,20},{18,22},{24,28},{26,30},{1,5},{... | collective-permute-start | bytes 3145736 | tf_op jit(solution)/shard_map/ppermute | solution.py:323
  44.3 1.0 copy-start.10
  65.7 16.3 %copy-start.11 = (bf16[2,512,512]{2,1,0:T(8,128)(2,1)}, bf16[2,512,512]{2,1,0:T(8,128)(2,1)S(1)}, u32[]{:S(2)}) copy-start(bf16[2,512,512]{2,1,0:T(8,128)(2,1)S(1)} %collective-permute-done.5.rest_0_.rest_5_) | copy-start | bytes 3145732
  71.7 10.3 %copy-start.12 = (bf16[2,512,512]{2,1,0:T(8,128)(2,1)}, bf16[2,512,512]{2,1,0:T(8,128)(2,1)S(1)}, u32[]{:S(2)}) copy-start(bf16[2,512,512]{2,1,0:T(8,128)(2,1)S(1)} %collective-permute-done.8.rest_4_.rest_9_) | copy-start | bytes 3145732
  74.7 7.3 %copy-start.13 = (bf16[2,512,512]{2,1,0:T(8,128)(2,1)}, bf16[2,512,512]{2,1,0:T(8,128)(2,1)S(1)}, u32[]{:S(2)}) copy-start(bf16[2,512,512]{2,1,0:T(8,128)(2,1)S(1)} %collective-permute-done.7.rest_5_.rest_10_) | copy-start | bytes 3145732
  74.7 5.3 %collective-permute-start.9 = (bf16[2,512,512]{2,1,0:T(8,128)(2,1)S(1)}, bf16[2,512,512]{2,1,0:T(8,128)(2,1)S(1)}, u32[]{:S(2)}, u32[]{:S(2)}) collective-permute-start(bf16[2,512,512]{2,1,0:T(8,128)(2,1)S(1)} %collective-permute-done.5.rest_0_.rest_5_), channel_id=1, source_target_pairs={{0,2},{2,0},{8,10},{10,8},{16,18},{18,16},{24,26},{26,24},{1,3},{3... | collective-permute-start | bytes 3145736 | tf_op jit(solution)/shard_map/ppermute | solution.py:323
  76.6 3.4 %collective-permute-start.10 = (bf16[2,512,512]{2,1,0:T(8,128)(2,1)}, bf16[2,512,512]{2,1,0:T(8,128)(2,1)S(1)}, u32[]{:S(2)}, u32[]{:S(2)}) collective-permute-start(bf16[2,512,512]{2,1,0:T(8,128)(2,1)} %collective-permute-done.6.rest_2_.rest_7_), channel_id=1, source_target_pairs={{4,6},{6,4},{12,14},{14,12},{20,22},{22,20},{28,30},{30,28},{5,7},... | collective-permute-start | bytes 3145736 | tf_op jit(solution)/shard_map/ppermute | solution.py:323
  77.3 4.7 %collective-permute-start.11 = (bf16[2,512,512]{2,1,0:T(8,128)(2,1)S(1)}, bf16[2,512,512]{2,1,0:T(8,128)(2,1)S(1)}, u32[]{:S(2)}, u32[]{:S(2)}) collective-permute-start(bf16[2,512,512]{2,1,0:T(8,128)(2,1)S(1)} %collective-permute-done.7.rest_5_.rest_10_), channel_id=1, source_target_pairs={{0,2},{2,0},{8,10},{10,8},{16,18},{18,16},{24,26},{26,24},{1,3},{3... | collective-permute-start | bytes 3145736 | tf_op jit(solution)/shard_map/ppermute | solution.py:323
  79.9 2.1 %copy-start.14 = (bf16[2,512,512]{2,1,0:T(8,128)(2,1)}, bf16[2,512,512]{2,1,0:T(8,128)(2,1)S(1)}, u32[]{:S(2)}) copy-start(bf16[2,512,512]{2,1,0:T(8,128)(2,1)S(1)} %collective-permute-done.9.rest_1_.rest_6_) | copy-start | bytes 3145732
  79.9 2.1 %copy-start.15 = (bf16[2,512,512]{2,1,0:T(8,128)(2,1)}, bf16[2,512,512]{2,1,0:T(8,128)(2,1)S(1)}, u32[]{:S(2)}) copy-start(bf16[2,512,512]{2,1,0:T(8,128)(2,1)S(1)} %collective-permute-done.10.rest_3_.rest_8_) | copy-start | bytes 3145732
  100.6 49.9 %collective-permute-start.14 = (bf16[256,2048]{1,0:T(8,128)(2,1)}, bf16[256,2048]{1,0:T(8,128)(2,1)S(1)}, u32[]{:S(2)}, u32[]{:S(2)}) collective-permute-start(bf16[256,2048]{1,0:T(8,128)(2,1)} %get-tuple-element.66), channel_id=1, source_target_pairs={{0,1},{1,0},{2,3},{3,2},{4,5},{5,4},{6,7},{7,6},{8,9},{9,8},{10,11... | collective-permute-start | bytes 3145736 | tf_op jit(solution)/shard_map/ppermute | solution.py:394
  101.9 1.4 copy-start.4
  114.9 37.8 %collective-permute-start.13 = (bf16[256,2048]{1,0:T(8,128)(2,1)S(1)}, bf16[256,2048]{1,0:T(8,128)(2,1)S(1)}, u32[]{:S(2)}, u32[]{:S(2)}) collective-permute-start(bf16[256,2048]{1,0:T(8,128)(2,1)S(1)} %get-tuple-element.65), channel_id=1, source_target_pairs={{0,1},{1,0},{2,3},{3,2},{4,5},{5,4},{6,7},{7,6},{8,9},{9,8},{10,11... | collective-permute-start | bytes 3145736 | tf_op jit(solution)/shard_map/ppermute | solution.py:396
  115.2 54.9 %collective-permute-start.12 = (bf16[256,2048]{1,0:T(8,128)(2,1)S(1)}, bf16[256,2048]{1,0:T(8,128)(2,1)S(1)}, u32[]{:S(2)}, u32[]{:S(2)}) collective-permute-start(bf16[256,2048]{1,0:T(8,128)(2,1)S(1)} %get-tuple-element.63), channel_id=1, source_target_pairs={{0,1},{1,0},{2,3},{3,2},{4,5},{5,4},{6,7},{7,6},{8,9},{9,8},{10,11... | collective-permute-start | bytes 3145736 | tf_op jit(solution)/shard_map/ppermute | solution.py:396
  142.4 1.4 copy-start.3
  143.8 6.8 %copy-start = (bf16[256,6144]{1,0:T(8,128)(2,1)S(1)}, bf16[256,6144]{1,0:T(8,128)(2,1)}, u32[]{:S(2)}) copy-start(bf16[256,6144]{1,0:T(8,128)(2,1)} %residual_ref.5) | copy-start | bytes 9437188
  143.8 6.8 %copy-start.1 = (bf16[256,4096]{1,0:T(8,128)(2,1)S(1)}, bf16[256,4096]{1,0:T(8,128)(2,1)}, u32[]{:S(2)}) copy-start(bf16[256,4096]{1,0:T(8,128)(2,1)} %get-tuple-element.64.rest_0_) | copy-start | bytes 6291460
  143.8 6.8 %copy-start.2 = (f32[32,6144]{1,0:T(8,128)S(1)}, f32[32,6144]{1,0:T(8,128)}, u32[]{:S(2)}) copy-start(f32[32,6144]{1,0:T(8,128)} %gate_ref.5) | copy-start | bytes 2359300
  143.8 6.8 %copy-start.5 = (s32[2]{0:T(128)S(1)}, s32[2]{0:T(128)}, u32[]{:S(2)}) copy-start(s32[2]{0:T(128)} %get-tuple-element.67.place) | copy-start | bytes 28
  143.8 6.8 %copy-start.6 = (s32[16]{0:T(128)S(1)}, s32[16]{0:T(128)}, u32[]{:S(2)}) copy-start(s32[16]{0:T(128)} %noise_step.5) | copy-start | bytes 196
  (1 other events, 1.0 us)

commit v4 on v3

--- a/solution.py
+++ b/solution.py
@@ -348,8 +348,7 @@
     hop = functools.partial(move, n_span=n_span)
     places = [jnp.stack([(my_head + k) % n_head, my_span]).astype(jnp.int32) for k in range(n_head)]
 
-    tile = model_width // 6
-    chunk = 2 * tile
+    chunk = model_width // 4
 
     def attend(k, blocks, state=None, columns=0, share=""):
         weight = out_weight if columns else None
@@ -392,17 +391,17 @@
         attended, partial = attend(k, late, states[k], chunk)
         route = [(i, (i + k) % n_head) for i in range(n_head)]
         begun = lax.ppermute(partial, "head", route)
-        partials = project(attended, out_weight, chunk, chunk, 2, tile)
+        partials = project(attended, out_weight, chunk, chunk, 3, chunk)
         received.append([begun] + [lax.ppermute(partial, "head", route) for partial in partials])
 
     states, attended = lax.optimization_barrier((states, attended))
-    attended, kept = attend(0, {**early, **late}, states[0], 2 * chunk, share="end")
-    (kept_end,) = project(attended, out_weight, 2 * chunk, chunk, 1, tile)
+    attended, kept = attend(0, {**early, **late}, states[0], 3 * chunk, share="end")
+    (kept_end,) = project(attended, out_weight, 3 * chunk, chunk, 1, chunk // 2)
     out = None
-    for c in range(3):
+    for c in range(4):
         parts = [got[c] for got in received]
-        at = (kept, c * chunk) if c < 2 else (kept_end, 0)
-        out = combine(places[0], noise_step, gate_table, residual, *at, parts, c * chunk, chunk, tile, out)
+        at = (kept, c * chunk) if c < 3 else (kept_end, 0)
+        out = combine(places[0], noise_step, gate_table, residual, *at, parts, c * chunk, chunk, chunk // 2, out)
     return out
 
 

time: 175 us -> 176 us (level)
  the two profiles are of different devices: /device:TPU:17 before, /device:TPU:24 now
where the time goes in v4:
time: 176 us; the launch traced here: 175 us
  Pallas kernels  130 us (74%)
  starting transfers between devices  24.5 us (14%)
  waiting for transfers between devices  12.3 us (7%)
  local copies, waits for them, and re-layouts  6.68 us (4%)
    pallas_call x6, Pallas kernels, attention(): pl.pallas_call(functools.partial(attention_kernel, slots, rows, group, fi...  104 us
    ppermute x12, starting transfers between devices, move(): return lax.ppermute(block, 'span', route)  20.3 us
    pallas_call x2, Pallas kernels, project(): pl.pallas_call(functools.partial(project_kernel, steps), out_shape=[jax.S...  18.4 us
    ppermute x12, waiting for transfers between devices, move(): return lax.ppermute(block, 'span', route)  12.3 us
    pallas_call x4, Pallas kernels, combine(): pl.pallas_call(functools.partial(combine_kernel, 1 + len(parts)), out_sha...  7.46 us
    unnamed x36, local copies, waits for them, and re-layouts  4.79 us
  transfers between devices with their start and end apart: 16, of which 4 were waited for; matrix products, arithmetic and copies ran while one was open for 0% of the time, Pallas kernels for 58%

profile of v4, /device:TPU:24, one launch (start us, length us, event | category | flops | bytes accessed | tf_op | source)
XLA Modules:
  0.0 175.0 jit_solution(8445208183963327414)
XLA Ops:
  0.0 1.2 reshape.3
  1.9 1.1 pad_maximum_fusion.rest_0_
  3.0 1.8 %collective-permute-start.2 = (bf16[2,512,512]{2,1,0:T(8,128)(2,1)}, bf16[2,512,512]{2,1,0:T(8,128)(2,1)S(1)}, u32[]{:S(2)}, u32[]{:S(2)}) collective-permute-start(bf16[2,512,512]{2,1,0:T(8,128)(2,1)} %pad_maximum_fusion.rest_0_), channel_id=1, source_target_pairs={{0,2},{4,6},{8,10},{12,14},{16,18},{20,22},{24,26},{28,30},{1,3},{... | collective-permute-start | bytes 3145736 | tf_op jit(solution)/shard_map/ppermute | solution.py:323
  4.8 1.6 collective-permute-start.1
  6.4 1.3 collective-permute-start
  8.3 9.2 %shard_map.83 = (f32[4,128,1536]{2,1,0:T(8,128)}, f32[4,8,1536]{2,1,0:T(8,128)}) custom-call(s32[2]{0:T(128)} %get-tuple-element.70.place, s32[16]{0:T(128)} %older_count.11, bf16[512,3072]{1,0:T(8,128)(2,1)} %q_ref.11, bf16[2,512,512]{2,1,0:T(8,128)(2,1)} %pad_maximum_fusion.rest_0_), custom_call_target="tpu_custom_call" | custom-call | tf_op jit(solution)/shard_map/pallas_call | solution.py:248
  17.5 9.2 %shard_map.82 = (f32[4,128,1536]{2,1,0:T(8,128)}, f32[4,8,1536]{2,1,0:T(8,128)}) custom-call(s32[2]{0:T(128)} %get-tuple-element.69.place, s32[16]{0:T(128)} %older_count.11, bf16[512,3072]{1,0:T(8,128)(2,1)} %q_ref.11, bf16[2,512,512]{2,1,0:T(8,128)(2,1)} %pad_maximum_fusion.rest_0_), custom_call_target="tpu_custom_call" | custom-call | tf_op jit(solution)/shard_map/pallas_call | solution.py:248
  26.7 2.7 %collective-permute-done.1.rest_1_ = bf16[2,512,512]{2,1,0:T(8,128)(2,1)S(1)} collective-permute-done((bf16[2,512,512]{2,1,0:T(8,128)(2,1)}, bf16[2,512,512]{2,1,0:T(8,128)(2,1)S(1)}, u32[]{:S(2)}, u32[]{:S(2)}) %collective-permute-start.1) | collective-permute-done | bytes 1048608 | tf_op jit(solution)/shard_map/ppermute | solution.py:323
  29.5 3.2 %collective-permute-done.rest_3_ = bf16[2,512,512]{2,1,0:T(8,128)(2,1)} collective-permute-done((bf16[2,512,512]{2,1,0:T(8,128)(2,1)}, bf16[2,512,512]{2,1,0:T(8,128)(2,1)}, u32[]{:S(2)}, u32[]{:S(2)}) %collective-permute-start) | collective-permute-done | bytes 1048608 | tf_op jit(solution)/shard_map/ppermute | solution.py:323
  33.5 1.3 collective-permute-start.5
  34.8 1.3 collective-permute-start.8
  36.1 1.3 collective-permute-start.7
  37.4 4.0 %collective-permute-start.6 = (bf16[2,512,512]{2,1,0:T(8,128)(2,1)}, bf16[2,512,512]{2,1,0:T(8,128)(2,1)}, u32[]{:S(2)}, u32[]{:S(2)}) collective-permute-start(bf16[2,512,512]{2,1,0:T(8,128)(2,1)} %collective-permute-done.rest_3_), channel_id=1, source_target_pairs={{0,4},{2,6},{8,12},{10,14},{16,20},{18,22},{24,28},{26,30},{1,5},{... | collective-permute-start | bytes 3145736 | tf_op jit(solution)/shard_map/ppermute | solution.py:323
  42.4 12.9 %shard_map.85 = (f32[4,128,1536]{2,1,0:T(8,128)}, f32[4,8,1536]{2,1,0:T(8,128)}) custom-call(s32[2]{0:T(128)} %get-tuple-element.70.place, s32[16]{0:T(128)} %older_count.11, bf16[512,3072]{1,0:T(8,128)(2,1)} %q_ref.11, bf16[2,512,512]{2,1,0:T(8,128)(2,1)} %copy-done.7, bf16[2,512,512]{2,1,0:T(8,128)(2,1)} %copy-done.8, bf16[2,512,512]{2,1,0:T(8,128)(2,1)} %copy-done.9, ...), custom_call_target="tpu_custom_call" | custom-call | tf_op jit(solution)/shard_map/pallas_call | solution.py:248
  55.3 13.0 %shard_map.84 = (f32[4,128,1536]{2,1,0:T(8,128)}, f32[4,8,1536]{2,1,0:T(8,128)}) custom-call(s32[2]{0:T(128)} %get-tuple-element.69.place, s32[16]{0:T(128)} %older_count.11, bf16[512,3072]{1,0:T(8,128)(2,1)} %q_ref.11, bf16[2,512,512]{2,1,0:T(8,128)(2,1)} %copy-done.7, bf16[2,512,512]{2,1,0:T(8,128)(2,1)} %copy-done.8, bf16[2,512,512]{2,1,0:T(8,128)(2,1)} %copy-done.9, ...), custom_call_target="tpu_custom_call" | custom-call | tf_op jit(solution)/shard_map/pallas_call | solution.py:248
  68.3 3.9 %collective-permute-done.8.rest_4_.rest_9_ = bf16[2,512,512]{2,1,0:T(8,128)(2,1)S(1)} collective-permute-done((bf16[2,512,512]{2,1,0:T(8,128)(2,1)}, bf16[2,512,512]{2,1,0:T(8,128)(2,1)S(1)}, u32[]{:S(2)}, u32[]{:S(2)}) %collective-permute-start.8) | collective-permute-done | bytes 1048608 | tf_op jit(solution)/shard_map/ppermute | solution.py:323
  72.2 4.2 %collective-permute-start.9 = (bf16[2,512,512]{2,1,0:T(8,128)(2,1)S(1)}, bf16[2,512,512]{2,1,0:T(8,128)(2,1)S(1)}, u32[]{:S(2)}, u32[]{:S(2)}) collective-permute-start(bf16[2,512,512]{2,1,0:T(8,128)(2,1)S(1)} %collective-permute-done.5.rest_0_.rest_5_), channel_id=1, source_target_pairs={{0,2},{2,0},{8,10},{10,8},{16,18},{18,16},{24,26},{26,24},{1,3},{3... | collective-permute-start | bytes 3145736 | tf_op jit(solution)/shard_map/ppermute | solution.py:323
  77.1 2.1 %collective-permute-start.11 = (bf16[2,512,512]{2,1,0:T(8,128)(2,1)S(1)}, bf16[2,512,512]{2,1,0:T(8,128)(2,1)S(1)}, u32[]{:S(2)}, u32[]{:S(2)}) collective-permute-start(bf16[2,512,512]{2,1,0:T(8,128)(2,1)S(1)} %collective-permute-done.7.rest_5_.rest_10_), channel_id=1, source_target_pairs={{0,2},{2,0},{8,10},{10,8},{16,18},{18,16},{24,26},{26,24},{1,3},{3... | collective-permute-start | bytes 3145736 | tf_op jit(solution)/shard_map/ppermute | solution.py:323
  79.3 2.4 %collective-permute-done.11.rest_6_.rest_11_ = bf16[2,512,512]{2,1,0:T(8,128)(2,1)S(1)} collective-permute-done((bf16[2,512,512]{2,1,0:T(8,128)(2,1)S(1)}, bf16[2,512,512]{2,1,0:T(8,128)(2,1)S(1)}, u32[]{:S(2)}, u32[]{:S(2)}) %collective-permute-start.11) | collective-permute-done | bytes 1048608 | tf_op jit(solution)/shard_map/ppermute | solution.py:323
  81.7 1.0 copy-done.16
  82.7 26.3 %shard_map.86 = (bf16[256,3072]{1,0:T(8,128)(2,1)}, bf16[256,1536]{1,0:T(8,128)(2,1)}) custom-call(s32[2]{0:T(128)} %get-tuple-element.70.place, s32[16]{0:T(128)} %older_count.11, bf16[512,3072]{1,0:T(8,128)(2,1)} %q_ref.11, bf16[2,512,512]{2,1,0:T(8,128)(2,1)} %copy-done.11, bf16[2,512,512]{2,1,0:T(8,128)(2,1)} %copy-done.14, ...), custom_call_target="tpu_custom_call" | custom-call | tf_op jit(solution)/shard_map/pallas_call | solution.py:248
  109.0 1.6 collective-permute-start.15
  110.5 1.4 copy-done.4
  111.9 12.9 %shard_map.89 = (bf16[256,1536]{1,0:T(8,128)(2,1)S(1)}, bf16[256,1536]{1,0:T(8,128)(2,1)S(1)}, bf16[256,1536]{1,0:T(8,128)(2,1)S(1)}) custom-call(bf16[256,3072]{1,0:T(8,128)(2,1)S(1)} %copy-done.4, bf16[3072,6144]{1,0:T(8,128)(2,1)} %w_ref.3), custom_call_target="tpu_custom_call" | custom-call | tf_op jit(solution)/shard_map/pallas_call | solution.py:275
  125.5 1.5 collective-permute-start.13
  127.5 33.0 %shard_map.87 = (bf16[256,3072]{1,0:T(8,128)(2,1)}, bf16[256,4608]{1,0:T(8,128)(2,1)}) custom-call(s32[2]{0:T(128)} %get-tuple-element.69.place, s32[16]{0:T(128)} %older_count.11, bf16[512,3072]{1,0:T(8,128)(2,1)} %q_ref.11, bf16[2,512,512]{2,1,0:T(8,128)(2,1)} %copy-done.7, bf16[2,512,512]{2,1,0:T(8,128)(2,1)} %copy-done.8, ...), custom_call_target="tpu_custom_call" | custom-call | tf_op jit(solution)/shard_map/pallas_call | solution.py:248
  160.6 1.4 copy-done.3
  162.0 5.5 %shard_map.88.rest_0_ = bf16[256,1536]{1,0:T(8,128)(2,1)S(1)} custom-call(bf16[256,3072]{1,0:T(8,128)(2,1)S(1)} %copy-done.3, bf16[3072,6144]{1,0:T(8,128)(2,1)} %w_ref.3), custom_call_target="tpu_custom_call" | custom-call | tf_op jit(solution)/shard_map/pallas_call | solution.py:275
  167.6 1.9 %shard_map.90.rest_2_ = bf16[256,6144]{1,0:T(8,128)(2,1)} custom-call(s32[2]{0:T(128)S(1)} %copy-done.5, s32[16]{0:T(128)S(1)} %copy-done.6, f32[32,6144]{1,0:T(8,128)S(1)} %copy-done.2, bf16[256,6144]{1,0:T(8,128)(2,1)S(1)} %copy-done, bf16[256,4608]{1,0:T(8,128)(2,1)S(1)} %copy-done.1, bf16[256,1536]{1,0:T(8,128)(2,1)S(1)} %collective-permute-done.15.rest_1_), custom_call_target="tpu_custom_call" | custom-call | tf_op jit(solution)/shard_map/pallas_call | solution.py:310
  169.4 1.9 %shard_map.91.rest_2_ = bf16[256,6144]{1,0:T(8,128)(2,1)} custom-call(s32[2]{0:T(128)S(1)} %copy-done.5, s32[16]{0:T(128)S(1)} %copy-done.6, f32[32,6144]{1,0:T(8,128)S(1)} %copy-done.2, bf16[256,6144]{1,0:T(8,128)(2,1)S(1)} %copy-done, bf16[256,4608]{1,0:T(8,128)(2,1)S(1)} %copy-done.1, ...), custom_call_target="tpu_custom_call", output_to_operand_aliasing={{}: (6, {})} | custom-call | tf_op jit(solution)/shard_map/pallas_call | solution.py:310
  171.3 1.9 %shard_map.92.rest_2_ = bf16[256,6144]{1,0:T(8,128)(2,1)} custom-call(s32[2]{0:T(128)S(1)} %copy-done.5, s32[16]{0:T(128)S(1)} %copy-done.6, f32[32,6144]{1,0:T(8,128)S(1)} %copy-done.2, bf16[256,6144]{1,0:T(8,128)(2,1)S(1)} %copy-done, bf16[256,4608]{1,0:T(8,128)(2,1)S(1)} %copy-done.1, ...), custom_call_target="tpu_custom_call", output_to_operand_aliasing={{}: (6, {})} | custom-call | tf_op jit(solution)/shard_map/pallas_call | solution.py:310
  173.2 1.9 %shard_map.93 = bf16[256,6144]{1,0:T(8,128)(2,1)} custom-call(s32[2]{0:T(128)S(1)} %copy-done.5, s32[16]{0:T(128)S(1)} %copy-done.6, f32[32,6144]{1,0:T(8,128)S(1)} %copy-done.2, bf16[256,6144]{1,0:T(8,128)(2,1)S(1)} %copy-done, bf16[256,1536]{1,0:T(8,128)(2,1)S(1)} %shard_map.88.rest_0_, ...), custom_call_target="tpu_custom_call", output_to_operand_aliasing={{}: (6, {})} | custom-call | tf_op jit(solution)/shard_map/pallas_call | solution.py:310
  (53 shorter events, 5.0 us)
Async XLA Ops:
  0.0 1.9 %copy-start.17 = (bf16[512,512]{1,0:T(8,128)(2,1)S(1)}, bf16[512,512]{1,0:T(8,128)(2,1)}, u32[]{:S(2)}) copy-start(bf16[512,512]{1,0:T(8,128)(2,1)} %param.9) | copy-start | bytes 1572868
  3.0 23.7 %collective-permute-start.2 = (bf16[2,512,512]{2,1,0:T(8,128)(2,1)}, bf16[2,512,512]{2,1,0:T(8,128)(2,1)S(1)}, u32[]{:S(2)}, u32[]{:S(2)}) collective-permute-start(bf16[2,512,512]{2,1,0:T(8,128)(2,1)} %pad_maximum_fusion.rest_0_), channel_id=1, source_target_pairs={{0,2},{4,6},{8,10},{12,14},{16,18},{20,22},{24,26},{28,30},{1,3},{... | collective-permute-start | bytes 3145736 | tf_op jit(solution)/shard_map/ppermute | solution.py:323
  4.8 24.7 %collective-permute-start.1 = (bf16[2,512,512]{2,1,0:T(8,128)(2,1)}, bf16[2,512,512]{2,1,0:T(8,128)(2,1)S(1)}, u32[]{:S(2)}, u32[]{:S(2)}) collective-permute-start(bf16[2,512,512]{2,1,0:T(8,128)(2,1)} %pad_maximum_fusion.rest_0_), channel_id=1, source_target_pairs={{0,4},{2,6},{4,0},{6,2},{8,12},{10,14},{12,8},{14,10},{16,20},{18,... | collective-permute-start | bytes 3145736 | tf_op jit(solution)/shard_map/ppermute | solution.py:323
  6.4 26.3 %collective-permute-start = (bf16[2,512,512]{2,1,0:T(8,128)(2,1)}, bf16[2,512,512]{2,1,0:T(8,128)(2,1)}, u32[]{:S(2)}, u32[]{:S(2)}) collective-permute-start(bf16[2,512,512]{2,1,0:T(8,128)(2,1)} %pad_maximum_fusion.rest_0_), channel_id=1, source_target_pairs={{0,8},{2,10},{4,12},{6,14},{8,16},{10,18},{12,20},{14,22},{16,24},... | collective-permute-start | bytes 3145736 | tf_op jit(solution)/shard_map/ppermute | solution.py:323
  26.7 14.7 %copy-start.7 = (bf16[2,512,512]{2,1,0:T(8,128)(2,1)}, bf16[2,512,512]{2,1,0:T(8,128)(2,1)S(1)}, u32[]{:S(2)}) copy-start(bf16[2,512,512]{2,1,0:T(8,128)(2,1)S(1)} %collective-permute-done.2.rest_0_) | copy-start | bytes 3145732
  29.5 11.9 %copy-start.8 = (bf16[2,512,512]{2,1,0:T(8,128)(2,1)}, bf16[2,512,512]{2,1,0:T(8,128)(2,1)S(1)}, u32[]{:S(2)}) copy-start(bf16[2,512,512]{2,1,0:T(8,128)(2,1)S(1)} %collective-permute-done.1.rest_1_) | copy-start | bytes 3145732
  32.7 4.7 %collective-permute-start.3 = (bf16[2,512,512]{2,1,0:T(8,128)(2,1)S(1)}, bf16[2,512,512]{2,1,0:T(8,128)(2,1)S(1)}, u32[]{:S(2)}, u32[]{:S(2)}) collective-permute-start(bf16[2,512,512]{2,1,0:T(8,128)(2,1)S(1)} %collective-permute-done.1.rest_1_), channel_id=1, source_target_pairs={{4,6},{6,4},{12,14},{14,12},{20,22},{22,20},{28,30},{30,28},{5,7},... | collective-permute-start | bytes 3145736 | tf_op jit(solution)/shard_map/ppermute | solution.py:323
  33.4 8.0 %collective-permute-start.4 = (bf16[2,512,512]{2,1,0:T(8,128)(2,1)}, bf16[2,512,512]{2,1,0:T(8,128)(2,1)S(1)}, u32[]{:S(2)}, u32[]{:S(2)}) collective-permute-start(bf16[2,512,512]{2,1,0:T(8,128)(2,1)} %collective-permute-done.rest_3_), channel_id=1, source_target_pairs={{0,2},{2,0},{4,6},{6,4},{8,10},{10,8},{12,14},{14,12},{16,18},{18,... | collective-permute-start | bytes 3145736 | tf_op jit(solution)/shard_map/ppermute | solution.py:323
  33.5 34.8 %collective-permute-start.5 = (bf16[2,512,512]{2,1,0:T(8,128)(2,1)S(1)}, bf16[2,512,512]{2,1,0:T(8,128)(2,1)S(1)}, u32[]{:S(2)}, u32[]{:S(2)}) collective-permute-start(bf16[2,512,512]{2,1,0:T(8,128)(2,1)S(1)} %collective-permute-done.1.rest_1_), channel_id=1, source_target_pairs={{0,8},{2,10},{8,16},{10,18},{16,24},{18,26},{1,9},{3,11},{9,17},{1... | collective-permute-start | bytes 3145736 | tf_op jit(solution)/shard_map/ppermute | solution.py:323
  34.8 37.4 %collective-permute-start.8 = (bf16[2,512,512]{2,1,0:T(8,128)(2,1)}, bf16[2,512,512]{2,1,0:T(8,128)(2,1)S(1)}, u32[]{:S(2)}, u32[]{:S(2)}) collective-permute-start(bf16[2,512,512]{2,1,0:T(8,128)(2,1)} %collective-permute-done.rest_3_), channel_id=1, source_target_pairs={{2,8},{6,12},{10,16},{14,20},{18,24},{22,28},{3,9},{7,13},{11,17},... | collective-permute-start | bytes 3145736 | tf_op jit(solution)/shard_map/ppermute | solution.py:323
  36.1 36.1 %collective-permute-start.7 = (bf16[2,512,512]{2,1,0:T(8,128)(2,1)}, bf16[2,512,512]{2,1,0:T(8,128)(2,1)S(1)}, u32[]{:S(2)}, u32[]{:S(2)}) collective-permute-start(bf16[2,512,512]{2,1,0:T(8,128)(2,1)} %collective-permute-done.rest_3_), channel_id=1, source_target_pairs={{4,8},{6,10},{12,16},{14,18},{20,24},{22,26},{5,9},{7,11},{13,17},... | collective-permute-start | bytes 3145736 | tf_op jit(solution)/shard_map/ppermute | solution.py:323
  37.4 4.0 %copy-start.9 = (bf16[2,512,512]{2,1,0:T(8,128)(2,1)}, bf16[2,512,512]{2,1,0:T(8,128)(2,1)S(1)}, u32[]{:S(2)}) copy-start(bf16[2,512,512]{2,1,0:T(8,128)(2,1)S(1)} %collective-permute-done.3.rest_2_) | copy-start | bytes 3145732
  37.4 34.8 %collective-permute-start.6 = (bf16[2,512,512]{2,1,0:T(8,128)(2,1)}, bf16[2,512,512]{2,1,0:T(8,128)(2,1)}, u32[]{:S(2)}, u32[]{:S(2)}) collective-permute-start(bf16[2,512,512]{2,1,0:T(8,128)(2,1)} %collective-permute-done.rest_3_), channel_id=1, source_target_pairs={{0,4},{2,6},{8,12},{10,14},{16,20},{18,22},{24,28},{26,30},{1,5},{... | collective-permute-start | bytes 3145736 | tf_op jit(solution)/shard_map/ppermute | solution.py:323
  68.3 13.4 %copy-start.11 = (bf16[2,512,512]{2,1,0:T(8,128)(2,1)}, bf16[2,512,512]{2,1,0:T(8,128)(2,1)S(1)}, u32[]{:S(2)}) copy-start(bf16[2,512,512]{2,1,0:T(8,128)(2,1)S(1)} %collective-permute-done.5.rest_0_.rest_5_) | copy-start | bytes 3145732
  72.2 9.5 %copy-start.12 = (bf16[2,512,512]{2,1,0:T(8,128)(2,1)}, bf16[2,512,512]{2,1,0:T(8,128)(2,1)S(1)}, u32[]{:S(2)}) copy-start(bf16[2,512,512]{2,1,0:T(8,128)(2,1)S(1)} %collective-permute-done.8.rest_4_.rest_9_) | copy-start | bytes 3145732
  72.2 9.5 %copy-start.13 = (bf16[2,512,512]{2,1,0:T(8,128)(2,1)}, bf16[2,512,512]{2,1,0:T(8,128)(2,1)S(1)}, u32[]{:S(2)}) copy-start(bf16[2,512,512]{2,1,0:T(8,128)(2,1)S(1)} %collective-permute-done.7.rest_5_.rest_10_) | copy-start | bytes 3145732
  72.2 7.0 %collective-permute-start.9 = (bf16[2,512,512]{2,1,0:T(8,128)(2,1)S(1)}, bf16[2,512,512]{2,1,0:T(8,128)(2,1)S(1)}, u32[]{:S(2)}, u32[]{:S(2)}) collective-permute-start(bf16[2,512,512]{2,1,0:T(8,128)(2,1)S(1)} %collective-permute-done.5.rest_0_.rest_5_), channel_id=1, source_target_pairs={{0,2},{2,0},{8,10},{10,8},{16,18},{18,16},{24,26},{26,24},{1,3},{3... | collective-permute-start | bytes 3145736 | tf_op jit(solution)/shard_map/ppermute | solution.py:323
  76.4 2.9 %collective-permute-start.10 = (bf16[2,512,512]{2,1,0:T(8,128)(2,1)}, bf16[2,512,512]{2,1,0:T(8,128)(2,1)S(1)}, u32[]{:S(2)}, u32[]{:S(2)}) collective-permute-start(bf16[2,512,512]{2,1,0:T(8,128)(2,1)} %collective-permute-done.6.rest_2_.rest_7_), channel_id=1, source_target_pairs={{4,6},{6,4},{12,14},{14,12},{20,22},{22,20},{28,30},{30,28},{5,7},... | collective-permute-start | bytes 3145736 | tf_op jit(solution)/shard_map/ppermute | solution.py:323
  77.1 4.6 %collective-permute-start.11 = (bf16[2,512,512]{2,1,0:T(8,128)(2,1)S(1)}, bf16[2,512,512]{2,1,0:T(8,128)(2,1)S(1)}, u32[]{:S(2)}, u32[]{:S(2)}) collective-permute-start(bf16[2,512,512]{2,1,0:T(8,128)(2,1)S(1)} %collective-permute-done.7.rest_5_.rest_10_), channel_id=1, source_target_pairs={{0,2},{2,0},{8,10},{10,8},{16,18},{18,16},{24,26},{26,24},{1,3},{3... | collective-permute-start | bytes 3145736 | tf_op jit(solution)/shard_map/ppermute | solution.py:323
  79.2 2.4 %copy-start.14 = (bf16[2,512,512]{2,1,0:T(8,128)(2,1)}, bf16[2,512,512]{2,1,0:T(8,128)(2,1)S(1)}, u32[]{:S(2)}) copy-start(bf16[2,512,512]{2,1,0:T(8,128)(2,1)S(1)} %collective-permute-done.9.rest_1_.rest_6_) | copy-start | bytes 3145732
  79.3 2.4 %copy-start.15 = (bf16[2,512,512]{2,1,0:T(8,128)(2,1)}, bf16[2,512,512]{2,1,0:T(8,128)(2,1)S(1)}, u32[]{:S(2)}) copy-start(bf16[2,512,512]{2,1,0:T(8,128)(2,1)S(1)} %collective-permute-done.10.rest_3_.rest_8_) | copy-start | bytes 3145732
  109.0 58.5 %collective-permute-start.15 = (bf16[256,1536]{1,0:T(8,128)(2,1)}, bf16[256,1536]{1,0:T(8,128)(2,1)S(1)}, u32[]{:S(2)}, u32[]{:S(2)}) collective-permute-start(bf16[256,1536]{1,0:T(8,128)(2,1)} %get-tuple-element.68), channel_id=1, source_target_pairs={{0,1},{1,0},{2,3},{3,2},{4,5},{5,4},{6,7},{7,6},{8,9},{9,8},{10,11... | collective-permute-start | bytes 2359304 | tf_op jit(solution)/shard_map/ppermute | solution.py:393
  110.5 1.4 copy-start.4
  124.9 44.5 %collective-permute-start.14 = (bf16[256,1536]{1,0:T(8,128)(2,1)S(1)}, bf16[256,1536]{1,0:T(8,128)(2,1)S(1)}, u32[]{:S(2)}, u32[]{:S(2)}) collective-permute-start(bf16[256,1536]{1,0:T(8,128)(2,1)S(1)} %get-tuple-element.67), channel_id=1, source_target_pairs={{0,1},{1,0},{2,3},{3,2},{4,5},{5,4},{6,7},{7,6},{8,9},{9,8},{10,11... | collective-permute-start | bytes 2359304 | tf_op jit(solution)/shard_map/ppermute | solution.py:395
  125.5 45.8 %collective-permute-start.13 = (bf16[256,1536]{1,0:T(8,128)(2,1)S(1)}, bf16[256,1536]{1,0:T(8,128)(2,1)S(1)}, u32[]{:S(2)}, u32[]{:S(2)}) collective-permute-start(bf16[256,1536]{1,0:T(8,128)(2,1)S(1)} %get-tuple-element.66), channel_id=1, source_target_pairs={{0,1},{1,0},{2,3},{3,2},{4,5},{5,4},{6,7},{7,6},{8,9},{9,8},{10,11... | collective-permute-start | bytes 2359304 | tf_op jit(solution)/shard_map/ppermute | solution.py:395
  127.0 46.2 %collective-permute-start.12 = (bf16[256,1536]{1,0:T(8,128)(2,1)S(1)}, bf16[256,1536]{1,0:T(8,128)(2,1)S(1)}, u32[]{:S(2)}, u32[]{:S(2)}) collective-permute-start(bf16[256,1536]{1,0:T(8,128)(2,1)S(1)} %get-tuple-element.64), channel_id=1, source_target_pairs={{0,1},{1,0},{2,3},{3,2},{4,5},{5,4},{6,7},{7,6},{8,9},{9,8},{10,11... | collective-permute-start | bytes 2359304 | tf_op jit(solution)/shard_map/ppermute | solution.py:395
  160.6 1.4 copy-start.3
  162.0 5.5 %copy-start = (bf16[256,6144]{1,0:T(8,128)(2,1)S(1)}, bf16[256,6144]{1,0:T(8,128)(2,1)}, u32[]{:S(2)}) copy-start(bf16[256,6144]{1,0:T(8,128)(2,1)} %residual_ref.7) | copy-start | bytes 9437188
  162.0 5.5 %copy-start.1 = (bf16[256,4608]{1,0:T(8,128)(2,1)S(1)}, bf16[256,4608]{1,0:T(8,128)(2,1)}, u32[]{:S(2)}) copy-start(bf16[256,4608]{1,0:T(8,128)(2,1)} %get-tuple-element.65.rest_0_) | copy-start | bytes 7077892
  162.0 5.6 %copy-start.2 = (f32[32,6144]{1,0:T(8,128)S(1)}, f32[32,6144]{1,0:T(8,128)}, u32[]{:S(2)}) copy-start(f32[32,6144]{1,0:T(8,128)} %gate_ref.7) | copy-start | bytes 2359300
  162.0 5.6 %copy-start.5 = (s32[2]{0:T(128)S(1)}, s32[2]{0:T(128)}, u32[]{:S(2)}) copy-start(s32[2]{0:T(128)} %get-tuple-element.69.place) | copy-start | bytes 28
  162.0 5.6 %copy-start.6 = (s32[16]{0:T(128)S(1)}, s32[16]{0:T(128)}, u32[]{:S(2)}) copy-start(s32[16]{0:T(128)} %noise_step.7) | copy-start | bytes 196
  (2 other events, 1.9 us)
